TPU v7x, 32 devices: a whole 2x2x4 slice. The times are simulated.
32 devices in a mesh: section: 4 (over y, x), seq: 8 (over z, core).
Axes of the slice: x: 2, y: 2, z: 4, core: 2. Of those that a mesh axis runs over, the one named last changes fastest.
Arguments:
- queries: bfloat16 [4, 2048, 2048], P('section', 'seq'), may hold values from -24 to 24
- keys: bfloat16 [4, 2048, 1024], P('section', 'seq'), may hold values from -24 to 24
- values: bfloat16 [4, 2048, 1024], P('section', 'seq'), may hold values from -6 to 6
- segment_ids: int32 [2048], P('seq'), may hold values from 0 to 3, as said below
- positions: int32 [2048], P('seq'), may hold values from 0 to 1023, as said below
- residual_in: bfloat16 [2048, 2048], P('seq'), may hold values from -6 to 6
- post_gain: float32 [4, 2048], P('section'), may hold values from 0.1 to 1.9
Outputs:
- layer_out: bfloat16 [4, 2048, 2048], P('section', 'seq')
Inputs may be any that keep to these rules, and one draw needn't show every extreme that they name: `segment_ids`: never falling; each document holds 1 to 1024 tokens, one exactly 1024. `positions`: the token's index minus the index of the first token of its document.
All inputs are finite; a program needn't handle non-finite values.
Results may differ from a plain program's by a relative error of at most 0.011.
Values may be sent and summed in bfloat16 or wider, within the bound.
A program may use at most 128 MiB of HBM per device.

v0:
```python
import math

import jax
import jax.numpy as jnp
from jax import lax
from jax.sharding import PartitionSpec as P

HQ = 8
HK = 4
HD = 256
WINDOW = 4096


def passed_along(value, axis, by):
    devices = lax.axis_size(axis)
    pairs = [(i, i + by) for i in range(devices) if 0 <= i + by < devices]
    return lax.ppermute(value, axis, pairs)


def carried_in(value, axis, join, neutral):
    count, mine = (lax.axis_size(axis), lax.axis_index(axis))
    pieces = lax.all_gather(value, axis)
    total = jnp.full_like(value, 0) + jnp.asarray(neutral, value.dtype)

    def turn(position, total):
        longer = join(total, pieces[position])
        return jnp.where(position < mine, longer, total)

    return lax.fori_loop(0, count - 1, turn, total)


def rotate(x, position, heads):
    count = x.shape[0]
    half = HD // 2
    parts = x.astype(jnp.float32).reshape(count, heads, HD)
    inverse = jnp.exp(-math.log(10000.0) * jnp.arange(half).astype(jnp.float32) / half)
    angle = position.astype(jnp.float32)[:, None] * inverse[None, :]
    cosine = jnp.cos(angle)[:, None, :]
    sine = jnp.sin(angle)[:, None, :]
    first = parts[:, :, :half]
    second = parts[:, :, half:]
    turned = jnp.concatenate(
        [first * cosine - second * sine, second * cosine + first * sine], axis=-1
    )
    return turned.reshape(count, heads * HD).astype(jnp.bfloat16)


def add_terms(earlier, later):
    return earlier + later


def per_device(queries, keys, values, segment_ids, positions, residual_in, post_gain):
    rows = segment_ids.shape[0]
    group = HQ // HK
    seq_count = lax.axis_size("seq")
    device = lax.axis_index("seq")
    local = jnp.arange(rows, dtype=jnp.int32)
    offset = device * rows
    query_rot = rotate(queries[0], positions, HQ)
    key_rot = rotate(keys[0], positions, HK)
    value_own = values[0]
    need = min((WINDOW + rows - 1) // rows, seq_count - 1) + 1
    key_buf = jnp.zeros((need, rows, HK * HD), jnp.bfloat16).at[0].set(key_rot)
    value_buf = jnp.zeros((need, rows, HK * HD), jnp.bfloat16).at[0].set(value_own)
    seg_buf = jnp.zeros((need, rows), jnp.int32).at[0].set(segment_ids)

    def relay_step(step, carry):
        current, buffers = carry
        current = passed_along((current[0], current[1], current[2]), "seq", 1)
        buffers = tuple(
            (
                lax.dynamic_update_index_in_dim(buf, piece, step, 0)
                for buf, piece in zip(buffers, current)
            )
        )
        return (current, buffers)

    carry_init = ((key_rot, value_own, segment_ids), (key_buf, value_buf, seg_buf))
    final_carry = lax.fori_loop(1, need, relay_step, carry_init)
    key_buf, value_buf, seg_buf = final_carry[1]
    query_grp = (
        query_rot.reshape(rows, HK, group, HD).transpose(1, 2, 0, 3).reshape(HK, group * rows, HD)
    )
    query_pos = offset + local
    scale = HD ** (-0.5)

    def attend(block, carry):
        key_blk = (
            lax.dynamic_index_in_dim(key_buf, block, 0, keepdims=False)
            .reshape(rows, HK, HD)
            .transpose(1, 0, 2)
        )
        value_blk = (
            lax.dynamic_index_in_dim(value_buf, block, 0, keepdims=False)
            .reshape(rows, HK, HD)
            .transpose(1, 0, 2)
        )
        seg_blk = lax.dynamic_index_in_dim(seg_buf, block, 0, keepdims=False)
        key_pos = (device - block) * rows + local
        numer, denom = carry
        score = (
            jnp.einsum("gqd,gkd->gqk", query_grp, key_blk, preferred_element_type=jnp.float32)
            * scale
        )
        score = 50.0 * jnp.tanh(score / 50.0)
        gap = query_pos[:, None] - key_pos[None, :]
        allowed = (
            (key_pos[None, :] >= 0)
            & (gap >= 0)
            & (gap < WINDOW)
            & (segment_ids[:, None] == seg_blk[None, :])
        )
        allowed = jnp.tile(allowed, (group, 1))
        weight = jnp.where(allowed[None], jnp.exp(score), 0.0)
        denom = denom + jnp.sum(weight, axis=-1)
        numer = numer + jnp.einsum(
            "gqk,gkd->gqd",
            weight.astype(jnp.bfloat16),
            value_blk,
            preferred_element_type=jnp.float32,
        )
        return (numer, denom)

    numer_init = jnp.zeros((HK, group * rows, HD), jnp.float32)
    denom_init = jnp.zeros((HK, group * rows), jnp.float32)
    numer, denom = lax.fori_loop(0, need, attend, (numer_init, denom_init))
    attended = (
        (numer / denom[..., None])
        .reshape(HK, group, rows, HD)
        .transpose(2, 0, 1, 3)
        .reshape(rows, HQ * HD)
    )
    norm = lax.rsqrt(jnp.mean(attended * attended, axis=-1, keepdims=True) + 1e-06)
    delta = attended * norm * post_gain[0][None, :]
    earlier = carried_in(delta, "section", add_terms, jnp.zeros_like(delta))
    running = residual_in.astype(jnp.float32) + earlier + delta
    return running.astype(jnp.bfloat16)[None]


def solution(mesh):
    placed = (
        P("section", "seq", None),
        P("section", "seq", None),
        P("section", "seq", None),
        P("seq"),
        P("seq"),
        P("seq", None),
        P("section", None),
    )
    return jax.shard_map(
        per_device, mesh=mesh, in_specs=placed, out_specs=P("section", "seq", None), check_vma=False
    )
```

profile of v0, /device:TPU:28, one launch (start us, length us, event | category | flops | bytes accessed | tf_op | source)
XLA Modules:
  0.0 354.0 jit_solution(17456105923690742711)
XLA Ops:
  13.0 2.5 scatter.10
  15.5 3.6 %scatter.11 = bf16[8,256,1024]{2,1,0:T(8,128)(2,1)} pad(bf16[1,256,1024]{2,1,0:T(8,128)(2,1)} %copy.86, bf16[]{:T(256)} %constant.239.clone.1), padding=0_7x0_0x0_0 | pad | bytes 4718594 | tf_op jit(solution)/shard_map/scatter | solution.py:64
  21.0 138.3 %while.58 = (s32[]{:T(128)}, bf16[256,1024]{1,0:T(8,128)(2,1)}, bf16[256,1024]{1,0:T(8,128)(2,1)}, s32[256]{0:T(256)S(1)}, bf16[8,256,1024]{2,1,0:T(8,128)(2,1)}...) while((s32[]{:T(128)}, bf16[256,1024]{1,0:T(8,128)(2,1)}, ...), condition=%wide.region_1.0_spmd, body=%wide.region_0.0_spmd.sunk | while | flops 5 | bytes 8397075 | solution.py:79
  22.9 1.9 collective-permute-start.1
  24.9 1.9 collective-permute-start.2
  26.8 10.6 %collective-permute-done.2 = s32[256]{0:T(256)S(1)} collective-permute-done((s32[256]{0:T(256)S(1)}, s32[256]{0:T(256)S(1)}, u32[]{:S(2)}, u32[]{:S(2)}) %collective-permute-start.2) | collective-permute-done | bytes 1056 | tf_op jit(solution)/shard_map/while/body/eval_jaxpr/ppermute | solution.py:17
  42.7 1.9 collective-permute-start.1
  44.6 1.9 collective-permute-start.2
  46.5 10.6 %collective-permute-done.2 = s32[256]{0:T(256)S(1)} collective-permute-done((s32[256]{0:T(256)S(1)}, s32[256]{0:T(256)S(1)}, u32[]{:S(2)}, u32[]{:S(2)}) %collective-permute-start.2) | collective-permute-done | bytes 1056 | tf_op jit(solution)/shard_map/while/body/eval_jaxpr/ppermute | solution.py:17
  62.5 1.9 collective-permute-start.1
  64.4 1.9 collective-permute-start.2
  66.3 10.6 %collective-permute-done.2 = s32[256]{0:T(256)S(1)} collective-permute-done((s32[256]{0:T(256)S(1)}, s32[256]{0:T(256)S(1)}, u32[]{:S(2)}, u32[]{:S(2)}) %collective-permute-start.2) | collective-permute-done | bytes 1056 | tf_op jit(solution)/shard_map/while/body/eval_jaxpr/ppermute | solution.py:17
  82.2 1.9 collective-permute-start.1
  84.1 1.9 collective-permute-start.2
  86.1 10.6 %collective-permute-done.2 = s32[256]{0:T(256)S(1)} collective-permute-done((s32[256]{0:T(256)S(1)}, s32[256]{0:T(256)S(1)}, u32[]{:S(2)}, u32[]{:S(2)}) %collective-permute-start.2) | collective-permute-done | bytes 1056 | tf_op jit(solution)/shard_map/while/body/eval_jaxpr/ppermute | solution.py:17
  102.0 1.9 collective-permute-start.1
  103.9 1.9 collective-permute-start.2
  105.8 10.6 %collective-permute-done.2 = s32[256]{0:T(256)S(1)} collective-permute-done((s32[256]{0:T(256)S(1)}, s32[256]{0:T(256)S(1)}, u32[]{:S(2)}, u32[]{:S(2)}) %collective-permute-start.2) | collective-permute-done | bytes 1056 | tf_op jit(solution)/shard_map/while/body/eval_jaxpr/ppermute | solution.py:17
  123.6 1.9 collective-permute-start.2
  125.6 10.6 %collective-permute-done.2 = s32[256]{0:T(256)S(1)} collective-permute-done((s32[256]{0:T(256)S(1)}, s32[256]{0:T(256)S(1)}, u32[]{:S(2)}, u32[]{:S(2)}) %collective-permute-start.2) | collective-permute-done | bytes 1056 | tf_op jit(solution)/shard_map/while/body/eval_jaxpr/ppermute | solution.py:17
  143.4 1.9 collective-permute-start.2
  145.3 10.6 %collective-permute-done.2 = s32[256]{0:T(256)S(1)} collective-permute-done((s32[256]{0:T(256)S(1)}, s32[256]{0:T(256)S(1)}, u32[]{:S(2)}, u32[]{:S(2)}) %collective-permute-start.2) | collective-permute-done | bytes 1056 | tf_op jit(solution)/shard_map/while/body/eval_jaxpr/ppermute | solution.py:17
  159.3 79.3 %while.59 = (s32[]{:T(128)}, f32[4,512,256]{2,1,0:T(8,128)S(1)}, f32[4,512]{1,0:T(4,128)S(1)}, s32[]{:T(128)}, s32[256]{0:T(256)S(1)}, /*index=5*/s32[8,256]{1,0...) while((s32[]{:T(128)}, f32[4,512,256]{2,1,0:T(8,128)S(1)}, ...), condition=%wide.region_4.5_spmd.clone, body=%wide.region_2.4_spmd.clone.sunk | while | flops 541002752 | bytes 15377076 | solution.py:126
  163.3 3.2 fusion.23
  166.9 2.2 select_add_fusion.4
  173.3 3.2 fusion.23
  176.8 2.2 select_add_fusion.4
  183.2 3.2 fusion.23
  186.7 2.2 select_add_fusion.4
  193.1 3.2 fusion.23
  196.6 2.2 select_add_fusion.4
  203.0 3.2 fusion.23
  206.6 2.2 select_add_fusion.4
  212.9 3.2 fusion.23
  216.5 2.2 select_add_fusion.4
  222.8 3.2 fusion.23
  226.4 2.2 select_add_fusion.4
  232.7 3.2 fusion.23
  236.3 2.2 select_add_fusion.4
  242.4 2.7 reshape.370
  245.1 3.2 multiply_multiply_fusion
  248.3 3.9 %reshape.371 = f32[256,2048]{1,0:T(8,128)} reshape(f32[256,4,2,256]{3,2,1,0:T(2,128)} %bitcast.72) | data formatting | bytes 4194304 | tf_op jit(solution)/shard_map/reshape | solution.py:131
  252.2 84.8 %all-gather.2.cloned.1.call-done = f32[4,256,2048]{2,1,0:T(8,128)} async-done(((f32[1,256,2048]{2,1,0:T(8,128)}), f32[4,256,2048]{2,1,0:T(8,128)}) %all-gather.2.cloned.1.call-update) | async-done | bytes 8388624 | tf_op jit(solution)/shard_map/all_gather | solution.py:22
  337.0 7.1 %while.60 = (s32[]{:T(128)}, f32[256,2048]{1,0:T(8,128)S(1)}, s32[]{:T(128)}, f32[4,256,2048]{2,1,0:T(8,128)}, s32[]{:T(128)}, /*index=5*/s32[]{:T(128)}) while((s32[]{:T(128)}, f32[256,2048]{1,0:T(8,128)S(1)}, s32[]{:T(128)}, f32[4,256,2048]{2,1,0:T(8,128)}, s32[]{:T(128)}, /*index=5*/s32[]{:T(128)}) %tuple.123), condition=%wide.region_7.8_spmd.clone, body=%wide.region_6.7_spmd.clone.sunk | while | flops 1572868 | bytes 6291549 | solution.py:29
  337.0 2.4 add_select_fusion.2
  339.4 2.3 add_select_fusion.2
  341.7 2.3 add_select_fusion.2
  344.0 3.1 fusion.10
  (196 shorter events, 88.5 us)
Async XLA Ops:
  6.5 330.4 %all-gather.2.cloned.1.call-start = ((), (), s32[]{:S(2)}) async-start(), calls=%async_computation | async-start | bytes 10485760 | tf_op jit(solution)/shard_map/all_gather | solution.py:22
  15.5 3.6 %copy-start.4 = (s32[256]{0:T(256)S(1)}, s32[256]{0:T(256)}, u32[]{:S(2)}) copy-start(s32[256]{0:T(256)} %param.22) | copy-start | bytes 3076
  15.5 3.6 %copy-start.3 = (s32[256]{0:T(256)S(1)}, s32[256]{0:T(256)}, u32[]{:S(2)}) copy-start(s32[256]{0:T(256)} %param.22) | copy-start | bytes 3076
  15.5 3.6 %copy-start.1 = (bf16[1,256,2048]{2,1,0:T(8,128)(2,1)S(1)}, bf16[1,256,2048]{2,1,0:T(8,128)(2,1)}, u32[]{:S(2)}) copy-start(bf16[1,256,2048]{2,1,0:T(8,128)(2,1)} %param.19) | copy-start | bytes 3145732
  21.0 16.4 %collective-permute-start = (bf16[256,1024]{1,0:T(8,128)(2,1)}, bf16[256,1024]{1,0:T(8,128)(2,1)S(1)}, u32[]{:S(2)}, u32[]{:S(2)}) collective-permute-start(bf16[256,1024]{1,0:T(8,128)(2,1)} %get-tuple-element.798), channel_id=1, source_target_pairs={{0,1},{1,2},{2,3},{3,4},{4,5},{5,6},{6,7},{8,9},{9,10},{10,11},{11... | collective-permute-start | bytes 1572872 | tf_op jit(solution)/shard_map/while/body/eval_jaxpr/ppermute | solution.py:17
  22.9 16.1 %collective-permute-start.1 = (bf16[256,1024]{1,0:T(8,128)(2,1)}, bf16[256,1024]{1,0:T(8,128)(2,1)S(1)}, u32[]{:S(2)}, u32[]{:S(2)}) collective-permute-start(bf16[256,1024]{1,0:T(8,128)(2,1)} %get-tuple-element.799), channel_id=1, source_target_pairs={{0,1},{1,2},{2,3},{3,4},{4,5},{5,6},{6,7},{8,9},{9,10},{10,11},{11... | collective-permute-start | bytes 1572872 | tf_op jit(solution)/shard_map/while/body/eval_jaxpr/ppermute | solution.py:17
  24.9 12.5 %collective-permute-start.2 = (s32[256]{0:T(256)S(1)}, s32[256]{0:T(256)S(1)}, u32[]{:S(2)}, u32[]{:S(2)}) collective-permute-start(s32[256]{0:T(256)S(1)} %get-tuple-element.800), channel_id=1, source_target_pairs={{0,1},{1,2},{2,3},{3,4},{4,5},{5,6},{6,7},{8,9},{9,10},{10,11},{11... | collective-permute-start | bytes 3080 | tf_op jit(solution)/shard_map/while/body/eval_jaxpr/ppermute | solution.py:17
  40.8 16.4 %collective-permute-start = (bf16[256,1024]{1,0:T(8,128)(2,1)}, bf16[256,1024]{1,0:T(8,128)(2,1)S(1)}, u32[]{:S(2)}, u32[]{:S(2)}) collective-permute-start(bf16[256,1024]{1,0:T(8,128)(2,1)} %get-tuple-element.798), channel_id=1, source_target_pairs={{0,1},{1,2},{2,3},{3,4},{4,5},{5,6},{6,7},{8,9},{9,10},{10,11},{11... | collective-permute-start | bytes 1572872 | tf_op jit(solution)/shard_map/while/body/eval_jaxpr/ppermute | solution.py:17
  42.7 16.2 %collective-permute-start.1 = (bf16[256,1024]{1,0:T(8,128)(2,1)}, bf16[256,1024]{1,0:T(8,128)(2,1)S(1)}, u32[]{:S(2)}, u32[]{:S(2)}) collective-permute-start(bf16[256,1024]{1,0:T(8,128)(2,1)} %get-tuple-element.799), channel_id=1, source_target_pairs={{0,1},{1,2},{2,3},{3,4},{4,5},{5,6},{6,7},{8,9},{9,10},{10,11},{11... | collective-permute-start | bytes 1572872 | tf_op jit(solution)/shard_map/while/body/eval_jaxpr/ppermute | solution.py:17
  44.6 12.5 %collective-permute-start.2 = (s32[256]{0:T(256)S(1)}, s32[256]{0:T(256)S(1)}, u32[]{:S(2)}, u32[]{:S(2)}) collective-permute-start(s32[256]{0:T(256)S(1)} %get-tuple-element.800), channel_id=1, source_target_pairs={{0,1},{1,2},{2,3},{3,4},{4,5},{5,6},{6,7},{8,9},{9,10},{10,11},{11... | collective-permute-start | bytes 3080 | tf_op jit(solution)/shard_map/while/body/eval_jaxpr/ppermute | solution.py:17
  60.6 16.4 %collective-permute-start = (bf16[256,1024]{1,0:T(8,128)(2,1)}, bf16[256,1024]{1,0:T(8,128)(2,1)S(1)}, u32[]{:S(2)}, u32[]{:S(2)}) collective-permute-start(bf16[256,1024]{1,0:T(8,128)(2,1)} %get-tuple-element.798), channel_id=1, source_target_pairs={{0,1},{1,2},{2,3},{3,4},{4,5},{5,6},{6,7},{8,9},{9,10},{10,11},{11... | collective-permute-start | bytes 1572872 | tf_op jit(solution)/shard_map/while/body/eval_jaxpr/ppermute | solution.py:17
  62.5 16.2 %collective-permute-start.1 = (bf16[256,1024]{1,0:T(8,128)(2,1)}, bf16[256,1024]{1,0:T(8,128)(2,1)S(1)}, u32[]{:S(2)}, u32[]{:S(2)}) collective-permute-start(bf16[256,1024]{1,0:T(8,128)(2,1)} %get-tuple-element.799), channel_id=1, source_target_pairs={{0,1},{1,2},{2,3},{3,4},{4,5},{5,6},{6,7},{8,9},{9,10},{10,11},{11... | collective-permute-start | bytes 1572872 | tf_op jit(solution)/shard_map/while/body/eval_jaxpr/ppermute | solution.py:17
  64.4 12.5 %collective-permute-start.2 = (s32[256]{0:T(256)S(1)}, s32[256]{0:T(256)S(1)}, u32[]{:S(2)}, u32[]{:S(2)}) collective-permute-start(s32[256]{0:T(256)S(1)} %get-tuple-element.800), channel_id=1, source_target_pairs={{0,1},{1,2},{2,3},{3,4},{4,5},{5,6},{6,7},{8,9},{9,10},{10,11},{11... | collective-permute-start | bytes 3080 | tf_op jit(solution)/shard_map/while/body/eval_jaxpr/ppermute | solution.py:17
  80.3 16.4 %collective-permute-start = (bf16[256,1024]{1,0:T(8,128)(2,1)}, bf16[256,1024]{1,0:T(8,128)(2,1)S(1)}, u32[]{:S(2)}, u32[]{:S(2)}) collective-permute-start(bf16[256,1024]{1,0:T(8,128)(2,1)} %get-tuple-element.798), channel_id=1, source_target_pairs={{0,1},{1,2},{2,3},{3,4},{4,5},{5,6},{6,7},{8,9},{9,10},{10,11},{11... | collective-permute-start | bytes 1572872 | tf_op jit(solution)/shard_map/while/body/eval_jaxpr/ppermute | solution.py:17
  82.2 16.2 %collective-permute-start.1 = (bf16[256,1024]{1,0:T(8,128)(2,1)}, bf16[256,1024]{1,0:T(8,128)(2,1)S(1)}, u32[]{:S(2)}, u32[]{:S(2)}) collective-permute-start(bf16[256,1024]{1,0:T(8,128)(2,1)} %get-tuple-element.799), channel_id=1, source_target_pairs={{0,1},{1,2},{2,3},{3,4},{4,5},{5,6},{6,7},{8,9},{9,10},{10,11},{11... | collective-permute-start | bytes 1572872 | tf_op jit(solution)/shard_map/while/body/eval_jaxpr/ppermute | solution.py:17
  84.1 12.5 %collective-permute-start.2 = (s32[256]{0:T(256)S(1)}, s32[256]{0:T(256)S(1)}, u32[]{:S(2)}, u32[]{:S(2)}) collective-permute-start(s32[256]{0:T(256)S(1)} %get-tuple-element.800), channel_id=1, source_target_pairs={{0,1},{1,2},{2,3},{3,4},{4,5},{5,6},{6,7},{8,9},{9,10},{10,11},{11... | collective-permute-start | bytes 3080 | tf_op jit(solution)/shard_map/while/body/eval_jaxpr/ppermute | solution.py:17
  100.0 16.4 %collective-permute-start = (bf16[256,1024]{1,0:T(8,128)(2,1)}, bf16[256,1024]{1,0:T(8,128)(2,1)S(1)}, u32[]{:S(2)}, u32[]{:S(2)}) collective-permute-start(bf16[256,1024]{1,0:T(8,128)(2,1)} %get-tuple-element.798), channel_id=1, source_target_pairs={{0,1},{1,2},{2,3},{3,4},{4,5},{5,6},{6,7},{8,9},{9,10},{10,11},{11... | collective-permute-start | bytes 1572872 | tf_op jit(solution)/shard_map/while/body/eval_jaxpr/ppermute | solution.py:17
  102.0 16.2 %collective-permute-start.1 = (bf16[256,1024]{1,0:T(8,128)(2,1)}, bf16[256,1024]{1,0:T(8,128)(2,1)S(1)}, u32[]{:S(2)}, u32[]{:S(2)}) collective-permute-start(bf16[256,1024]{1,0:T(8,128)(2,1)} %get-tuple-element.799), channel_id=1, source_target_pairs={{0,1},{1,2},{2,3},{3,4},{4,5},{5,6},{6,7},{8,9},{9,10},{10,11},{11... | collective-permute-start | bytes 1572872 | tf_op jit(solution)/shard_map/while/body/eval_jaxpr/ppermute | solution.py:17
  103.9 12.5 %collective-permute-start.2 = (s32[256]{0:T(256)S(1)}, s32[256]{0:T(256)S(1)}, u32[]{:S(2)}, u32[]{:S(2)}) collective-permute-start(s32[256]{0:T(256)S(1)} %get-tuple-element.800), channel_id=1, source_target_pairs={{0,1},{1,2},{2,3},{3,4},{4,5},{5,6},{6,7},{8,9},{9,10},{10,11},{11... | collective-permute-start | bytes 3080 | tf_op jit(solution)/shard_map/while/body/eval_jaxpr/ppermute | solution.py:17
  119.8 16.4 %collective-permute-start = (bf16[256,1024]{1,0:T(8,128)(2,1)}, bf16[256,1024]{1,0:T(8,128)(2,1)S(1)}, u32[]{:S(2)}, u32[]{:S(2)}) collective-permute-start(bf16[256,1024]{1,0:T(8,128)(2,1)} %get-tuple-element.798), channel_id=1, source_target_pairs={{0,1},{1,2},{2,3},{3,4},{4,5},{5,6},{6,7},{8,9},{9,10},{10,11},{11... | collective-permute-start | bytes 1572872 | tf_op jit(solution)/shard_map/while/body/eval_jaxpr/ppermute | solution.py:17
  121.7 16.1 %collective-permute-start.1 = (bf16[256,1024]{1,0:T(8,128)(2,1)}, bf16[256,1024]{1,0:T(8,128)(2,1)S(1)}, u32[]{:S(2)}, u32[]{:S(2)}) collective-permute-start(bf16[256,1024]{1,0:T(8,128)(2,1)} %get-tuple-element.799), channel_id=1, source_target_pairs={{0,1},{1,2},{2,3},{3,4},{4,5},{5,6},{6,7},{8,9},{9,10},{10,11},{11... | collective-permute-start | bytes 1572872 | tf_op jit(solution)/shard_map/while/body/eval_jaxpr/ppermute | solution.py:17
  123.6 12.5 %collective-permute-start.2 = (s32[256]{0:T(256)S(1)}, s32[256]{0:T(256)S(1)}, u32[]{:S(2)}, u32[]{:S(2)}) collective-permute-start(s32[256]{0:T(256)S(1)} %get-tuple-element.800), channel_id=1, source_target_pairs={{0,1},{1,2},{2,3},{3,4},{4,5},{5,6},{6,7},{8,9},{9,10},{10,11},{11... | collective-permute-start | bytes 3080 | tf_op jit(solution)/shard_map/while/body/eval_jaxpr/ppermute | solution.py:17
  139.5 16.4 %collective-permute-start = (bf16[256,1024]{1,0:T(8,128)(2,1)}, bf16[256,1024]{1,0:T(8,128)(2,1)S(1)}, u32[]{:S(2)}, u32[]{:S(2)}) collective-permute-start(bf16[256,1024]{1,0:T(8,128)(2,1)} %get-tuple-element.798), channel_id=1, source_target_pairs={{0,1},{1,2},{2,3},{3,4},{4,5},{5,6},{6,7},{8,9},{9,10},{10,11},{11... | collective-permute-start | bytes 1572872 | tf_op jit(solution)/shard_map/while/body/eval_jaxpr/ppermute | solution.py:17
  141.4 16.1 %collective-permute-start.1 = (bf16[256,1024]{1,0:T(8,128)(2,1)}, bf16[256,1024]{1,0:T(8,128)(2,1)S(1)}, u32[]{:S(2)}, u32[]{:S(2)}) collective-permute-start(bf16[256,1024]{1,0:T(8,128)(2,1)} %get-tuple-element.799), channel_id=1, source_target_pairs={{0,1},{1,2},{2,3},{3,4},{4,5},{5,6},{6,7},{8,9},{9,10},{10,11},{11... | collective-permute-start | bytes 1572872 | tf_op jit(solution)/shard_map/while/body/eval_jaxpr/ppermute | solution.py:17
  143.4 12.5 %collective-permute-start.2 = (s32[256]{0:T(256)S(1)}, s32[256]{0:T(256)S(1)}, u32[]{:S(2)}, u32[]{:S(2)}) collective-permute-start(s32[256]{0:T(256)S(1)} %get-tuple-element.800), channel_id=1, source_target_pairs={{0,1},{1,2},{2,3},{3,4},{4,5},{5,6},{6,7},{8,9},{9,10},{10,11},{11... | collective-permute-start | bytes 3080 | tf_op jit(solution)/shard_map/while/body/eval_jaxpr/ppermute | solution.py:17
  240.5 4.5 %copy-start = (f32[4,2,256,256]{3,1,0,2:T(2,128)}, f32[4,2,256,256]{3,1,0,2:T(2,128)S(1)}, u32[]{:S(2)}) copy-start(f32[4,2,256,256]{3,1,0,2:T(2,128)S(1)} %copy.35) | copy-start | bytes 6291460
  242.4 2.7 copy-start.5
  337.0 7.1 %copy-start.2 = (bf16[256,2048]{1,0:T(8,128)(2,1)S(1)}, bf16[256,2048]{1,0:T(8,128)(2,1)}, u32[]{:S(2)}) copy-start(bf16[256,2048]{1,0:T(8,128)(2,1)} %param.24) | copy-start | bytes 3145732
Sparse Core Ops, SparseCore 0:
  248.4 88.5 all-gather.1
where the time goes:
time: 358 us; the launch traced here: 354 us
  waiting for transfers between devices  159 us (44%)
  local copies, waits for them, and re-layouts  78 us (22%)
  matrix products  43 us (12%)
  starting transfers between devices  40.2 us (11%)
  other arithmetic  19.3 us (5%)
  between operations  13.5 us (4%)
    all_gather x1, waiting for transfers between devices, carried_in(): pieces = lax.all_gather(value, axis)  84.8 us
    ppermute x21, waiting for transfers between devices, passed_along(): return lax.ppermute(value, axis, pairs)  74.1 us
    ppermute x21, starting transfers between devices, passed_along(): return lax.ppermute(value, axis, pairs)  40.2 us
    dot_general x8, matrix products, attend(): jnp.einsum('gqd,gkd->gqk', query_grp, key_blk, preferred_element_type=jnp...  25.2 us
    dot_general x8, matrix products, attend(): jnp.einsum('gqk,gkd->gqd', weight.astype(jnp.bfloat16), value_blk, prefer...  17.8 us
    dynamic_update_slice x21, local copies, waits for them, and re-layouts, relay_step(): lax.dynamic_update_index_in_dim(buf, piece, step, 0)  12 us
    dynamic_slice x16, local copies, waits for them, and re-layouts, attend(): lax.dynamic_index_in_dim(value_buf, block, 0, keepdims=False)  11.8 us
    while x21, local copies, waits for them, and re-layouts  11.6 us
  transfers between devices with their start and end apart: 22, of which 8 were waited for; matrix products, arithmetic and copies ran while one was open for 4% of the time, Pallas kernels for 0%

commit v1 on v0

v1 whole, which is shorter than its diff:
```python
import functools
import math

import jax
import jax.numpy as jnp
from jax import lax
from jax.experimental import pallas as pl
from jax.experimental.pallas import tpu as pltpu
from jax.sharding import PartitionSpec as P

HQ = 8
HK = 4
HD = 256
WINDOW = 4096
GROUP = HQ // HK
HALF = HD // 2
PAIR = GROUP * HD
MESH = pl.DeviceIdType.MESH
NT = (((1,), (1,)), ((), ()))
NN = (((1,), (0,)), ((), ()))


def kernel(
    seqs, secs, back, rows,
    q_ref, k_ref, v_ref, pos_ref, res_ref, gain_ref,
    out_ref,
    kv, qrot, cos_ref, sin_ref, low, acc, den, own, sent, got, gains,
    kv_send, kv_recv, att_send, att_recv, gain_send, gain_recv,
):
    me = lax.axis_index("seq")
    sec = lax.axis_index("section")

    barrier = pltpu.get_barrier_semaphore()

    @pl.when(me > 0)
    def _():
        pl.semaphore_signal(barrier, inc=1, device_id={"seq": me - 1}, device_id_type=MESH)

    for other in range(secs - 1):

        @pl.when(other < sec)
        def _(other=other):
            pl.semaphore_signal(barrier, inc=1, device_id={"section": other}, device_id_type=MESH)

    def kv_copy(step, head):
        return pltpu.make_async_remote_copy(
            src_ref=kv.at[step, head],
            dst_ref=kv.at[step + 1, head],
            send_sem=kv_send.at[step, head],
            recv_sem=kv_recv.at[step, head],
            device_id={"seq": me + 1},
            device_id_type=MESH,
        )

    def att_copy(source, head, target):
        return pltpu.make_async_remote_copy(
            src_ref=sent.at[head],
            dst_ref=got.at[source, head],
            send_sem=att_send.at[target - 1, head],
            recv_sem=att_recv.at[source, head],
            device_id={"section": target},
            device_id_type=MESH,
        )

    def gain_copy(source, target):
        return pltpu.make_async_remote_copy(
            src_ref=gains.at[secs - 1],
            dst_ref=gains.at[source],
            send_sem=gain_send.at[target - 1],
            recv_sem=gain_recv.at[source],
            device_id={"section": target},
            device_id_type=MESH,
        )

    def to_later(act):
        for target in range(1, secs):

            @pl.when(target > sec)
            def _(target=target):
                act(target)

    place = jnp.broadcast_to(pos_ref[...], (HALF, rows)).astype(jnp.float32).T
    lane = lax.broadcasted_iota(jnp.int32, (rows, HALF), 1).astype(jnp.float32)
    angle = place * jnp.exp(lane * (-math.log(10000.0) / HALF))
    cos_ref[...] = jnp.cos(angle)
    sin_ref[...] = jnp.sin(angle)
    gains[secs - 1] = jnp.broadcast_to(gain_ref[...], gains.shape[1:])

    def turned(ref, head):
        first = ref[0, :, head * HD : head * HD + HALF].astype(jnp.float32)
        second = ref[0, :, head * HD + HALF : (head + 1) * HD].astype(jnp.float32)
        cosine, sine = cos_ref[...], sin_ref[...]
        return (
            (first * cosine - second * sine).astype(jnp.bfloat16),
            (second * cosine + first * sine).astype(jnp.bfloat16),
        )

    def pack(head):
        first, second = turned(k_ref, head)
        kv[0, head, :, :HALF] = first
        kv[0, head, :, HALF:HD] = second
        kv[0, head, :, HD:] = v_ref[0, :, head * HD : (head + 1) * HD]

    pack(0)
    expected = jnp.where(me < seqs - 1, 1, 0) + (secs - 1 - sec)

    @pl.when(expected > 0)
    def _():
        pl.semaphore_wait(barrier, expected)

    @pl.when(me < seqs - 1)
    def _():
        kv_copy(0, 0).start()

    to_later(lambda target: gain_copy(sec, target).start())

    for head in range(1, HK):
        pack(head)
    for head in range(HQ):
        first, second = turned(q_ref, head)
        part = pl.ds((head % GROUP) * rows, rows)
        qrot[head // GROUP, part, :HALF] = first
        qrot[head // GROUP, part, HALF:] = second

    reach = jnp.minimum(place, float(WINDOW - 1)).astype(jnp.int32)
    gap = lax.broadcasted_iota(jnp.int32, (rows, rows), 0) - lax.broadcasted_iota(
        jnp.int32, (rows, rows), 1
    )
    for start in range(0, rows, HALF):
        low[:, start : start + HALF] = gap[:, start : start + HALF] - reach

    def block(step, head, first):
        for part in range(GROUP):
            at = pl.ds(part * rows, rows)
            score = lax.dot_general(
                qrot[head, at, :], kv[step, head, :, :HD], NT, preferred_element_type=jnp.float32
            )
            capped = jnp.tanh(score * (HD ** (-0.5) / 50.0))
            weight = jnp.exp2(capped * (50.0 * math.log2(math.e)))
            allowed = low[...] <= -step * rows
            if first:
                allowed = allowed & (gap >= 0)
            weight = jnp.where(allowed, weight, 0.0)
            total = weight[:, :HALF]
            for start in range(HALF, rows, HALF):
                total = total + weight[:, start : start + HALF]
            summed = lax.dot_general(
                weight.astype(jnp.bfloat16),
                kv[step, head, :, HD:],
                NN,
                preferred_element_type=jnp.float32,
            )
            if first:
                den[at, :] = total
                acc[at, :] = summed
            else:
                den[at, :] += total
                acc[at, :] += summed

    def one_head(head, carry):
        block(0, head, True)

        def earlier(step, carry):
            @pl.when((step == back) & (head < HK - 1) & (me < seqs - 1))
            def _():
                kv_copy(0, head + 1).start()

            @pl.when(me >= step)
            def _():
                kv_copy(step - 1, head).wait_recv()

                @pl.when((step < back) & (me < seqs - 1))
                def _():
                    kv_copy(step, head).start()

                block(step, head, False)

            return carry

        lax.fori_loop(1, back + 1, earlier, 0)
        for part in range(GROUP):
            at = pl.ds(part * rows, rows)
            cols = pl.ds(part * HD, HD)
            value = acc[at, :] / jnp.sum(den[at, :], axis=-1, keepdims=True)
            own[head, :, cols] = value
            sent[head, :, cols] = value.astype(jnp.bfloat16)
        to_later(lambda target: att_copy(sec, head, target).start())
        return carry

    lax.fori_loop(0, HK, one_head, 0)

    def norm_of(parts):
        square = 0.0
        for head in range(HK):
            value = parts(head)
            square = square + jnp.sum(value * value, axis=-1, keepdims=True)
        return lax.rsqrt(square * (1.0 / (HQ * HD)) + 1e-06)

    norm = norm_of(lambda head: own[head])
    for head in range(HK):
        cols = slice(head * PAIR, (head + 1) * PAIR)
        own[head] = own[head] * norm * gains[secs - 1, :1, cols] + res_ref[:, cols].astype(
            jnp.float32
        )

    for source in range(secs - 1):

        @pl.when(source < sec)
        def _(source=source):
            gain_copy(source, secs - 1).wait_recv()
            for head in range(HK):
                att_copy(source, head, secs - 1).wait_recv()
            norm = norm_of(lambda head: got[source, head].astype(jnp.float32))
            for head in range(HK):
                cols = slice(head * PAIR, (head + 1) * PAIR)
                own[head] += got[source, head].astype(jnp.float32) * norm * gains[source, :1, cols]

    for head in range(HK):
        out_ref[0, :, head * PAIR : (head + 1) * PAIR] = own[head].astype(jnp.bfloat16)

    def finish_head(head, carry):
        def finish_step(step, carry):
            @pl.when((me >= step) & (me < seqs - 1))
            def _():
                kv_copy(step, head).wait_send()

            return carry

        lax.fori_loop(0, back, finish_step, 0)
        to_later(lambda target: att_copy(sec, head, target).wait_send())
        return carry

    lax.fori_loop(0, HK, finish_head, 0)
    to_later(lambda target: gain_copy(sec, target).wait_send())


def per_device(queries, keys, values, segment_ids, positions, residual_in, post_gain):
    rows = positions.shape[0]
    seqs = lax.axis_size("seq")
    secs = lax.axis_size("section")
    longest = seqs * rows // 2
    back = min((min(WINDOW, longest) - 1 + rows - 1) // rows, seqs - 1)
    vmem = pl.BlockSpec(memory_space=pltpu.VMEM)
    return pl.pallas_call(
        functools.partial(kernel, seqs, secs, back, rows),
        out_shape=jax.ShapeDtypeStruct((1, rows, HQ * HD), jnp.bfloat16),
        in_specs=[vmem] * 6,
        out_specs=vmem,
        scratch_shapes=[
            pltpu.VMEM((back + 1, HK, rows, 2 * HD), jnp.bfloat16),
            pltpu.VMEM((HK, GROUP * rows, HD), jnp.bfloat16),
            pltpu.VMEM((rows, HALF), jnp.float32),
            pltpu.VMEM((rows, HALF), jnp.float32),
            pltpu.VMEM((rows, rows), jnp.int32),
            pltpu.VMEM((GROUP * rows, HD), jnp.float32),
            pltpu.VMEM((GROUP * rows, HALF), jnp.float32),
            pltpu.VMEM((HK, rows, PAIR), jnp.float32),
            pltpu.VMEM((HK, rows, PAIR), jnp.bfloat16),
            pltpu.VMEM((secs - 1, HK, rows, PAIR), jnp.bfloat16),
            pltpu.VMEM((secs, 8, HQ * HD), jnp.float32),
            pltpu.SemaphoreType.DMA((back, HK)),
            pltpu.SemaphoreType.DMA((back, HK)),
            pltpu.SemaphoreType.DMA((secs - 1, HK)),
            pltpu.SemaphoreType.DMA((secs - 1, HK)),
            pltpu.SemaphoreType.DMA((secs - 1,)),
            pltpu.SemaphoreType.DMA((secs - 1,)),
        ],
        compiler_params=pltpu.CompilerParams(
            collective_id=0, has_side_effects=True, vmem_limit_bytes=52 * 2**20
        ),
    )(queries, keys, values, positions.reshape(1, rows), residual_in, post_gain)


def solution(mesh):
    placed = (
        P("section", "seq", None),
        P("section", "seq", None),
        P("section", "seq", None),
        P("seq"),
        P("seq"),
        P("seq", None),
        P("section", None),
    )
    return jax.shard_map(
        per_device, mesh=mesh, in_specs=placed, out_specs=P("section", "seq", None), check_vma=False
    )
```

time: 358 us -> 71.3 us (0.20)
  waiting for transfers between devices: 159 us -> 0 us
  local copies, waits for them, and re-layouts: 78 us -> 5.76 us
  Pallas kernels: 0 us -> 64.7 us
  matrix products: 43 us -> 0 us
  starting transfers between devices: 40.2 us -> 0 us
  other arithmetic: 19.3 us -> 0 us
  between operations: 13.5 us -> 0.01 us
    all_gather x1 -> x0, waiting for transfers between devices: 84.8 us -> none  [carried_in(): pieces = lax.all_gather(value, axis)]
    ppermute x21 -> x0, waiting for transfers between devices: 74.1 us -> none  [passed_along(): return lax.ppermute(value, axis, pairs)]
    pallas_call x0 -> x1, Pallas kernels: none -> 64.7 us  [per_device(): pl.pallas_call(functools.partial(kernel, seqs, secs, back, rows), out_sha...]
    dot_general x16 -> x0, matrix products: 43 us -> none  [the longest x8 25.2 us: attend(): jnp.einsum('gqd,gkd->gqk', query_grp, key_blk, preferred_element_type=jnp...]
    ppermute x21 -> x0, starting transfers between devices: 40.2 us -> none  [passed_along(): return lax.ppermute(value, axis, pairs)]
    dynamic_slice x32 -> x0, local copies, waits for them, and re-layouts: 20.2 us -> none  [the longest x16 11.8 us: attend(): lax.dynamic_index_in_dim(value_buf, block, 0, keepdims=False)]
    reshape x19 -> x0, local copies, waits for them, and re-layouts: 19.7 us -> none  [the longest x8 9.94 us: attend(): key_blk = lax.dynamic_index_in_dim(key_buf, block, 0, keepdims=False).res...]
    dynamic_update_slice x21 -> x0, local copies, waits for them, and re-layouts: 12 us -> none  [relay_step(): lax.dynamic_update_index_in_dim(buf, piece, step, 0)]
  transfers between devices with their start and end apart: 22 -> 0, of which waited for: 8 -> 0; matrix products, arithmetic and copies ran while one was open for 4% -> 0% of each run, Pallas kernels for 0% -> 0%
where the time goes in v1:
time: 71.3 us; the launch traced here: 70.5 us
  Pallas kernels  64.7 us (91%)
  local copies, waits for them, and re-layouts  5.76 us (8%)
    pallas_call x1, Pallas kernels, per_device(): pl.pallas_call(functools.partial(kernel, seqs, secs, back, rows), out_sha...  64.7 us
    unnamed x9, local copies, waits for them, and re-layouts  5.76 us

profile of v1, /device:TPU:28, one launch (start us, length us, event | category | flops | bytes accessed | tf_op | source)
XLA Modules:
  0.0 70.5 jit_solution(17021025474499158469)
XLA Ops:
  0.0 0.0 copy-start.3
  0.0 0.7 copy-done.3
  0.7 0.0 copy-start
  0.7 1.0 %copy-done = bf16[1,256,1024]{2,1,0:T(8,128)(2,1)S(1)} copy-done((bf16[1,256,1024]{2,1,0:T(8,128)(2,1)S(1)}, bf16[1,256,1024]{2,1,0:T(8,128)(2,1)}, u32[]{:S(2)}) %copy-start) | copy-done | bytes 524312
  1.7 0.0 copy-start.1
  1.7 1.0 %copy-done.1 = bf16[1,256,1024]{2,1,0:T(8,128)(2,1)S(1)} copy-done((bf16[1,256,1024]{2,1,0:T(8,128)(2,1)S(1)}, bf16[1,256,1024]{2,1,0:T(8,128)(2,1)}, u32[]{:S(2)}) %copy-start.1) | copy-done | bytes 524312
  2.8 0.0 copy-start.2
  2.8 0.7 copy-done.2
  3.5 64.7 %shard_map.64 = bf16[1,256,2048]{2,1,0:T(8,128)(2,1)} custom-call(bf16[1,256,2048]{2,1,0:T(8,128)(2,1)} %q_ref.1, bf16[1,256,1024]{2,1,0:T(8,128)(2,1)S(1)} %copy-done, bf16[1,256,1024]{2,1,0:T(8,128)(2,1)S(1)} %copy-done.1, s32[1,256]{1,0:T(1,128)S(1)} %bitcast.1, bf16[256,2048]{1,0:T(8,128)(2,1)} %res_ref.1, f32[1,2048]{1,0:T(1,128)S(1)} %copy-done.2), custom_call_target="tpu_custom_call" | custom-call | tf_op jit(solution)/shard_map/pallas_call | solution.py:244
  68.2 2.3 %copy.8 = bf16[1,256,2048]{2,1,0:T(8,128)(2,1)} copy(bf16[1,256,2048]{2,1,0:T(8,128)(2,1)} %shard_map.64) | data formatting | bytes 2097152
Async XLA Ops:
  0.0 0.7 copy-start.3
  0.7 1.0 %copy-start = (bf16[1,256,1024]{2,1,0:T(8,128)(2,1)S(1)}, bf16[1,256,1024]{2,1,0:T(8,128)(2,1)}, u32[]{:S(2)}) copy-start(bf16[1,256,1024]{2,1,0:T(8,128)(2,1)} %k_ref.1) | copy-start | bytes 1572868
  1.7 1.0 %copy-start.1 = (bf16[1,256,1024]{2,1,0:T(8,128)(2,1)S(1)}, bf16[1,256,1024]{2,1,0:T(8,128)(2,1)}, u32[]{:S(2)}) copy-start(bf16[1,256,1024]{2,1,0:T(8,128)(2,1)} %v_ref.1) | copy-start | bytes 1572868
  2.8 0.7 copy-start.2

commit v2 on v1

--- a/solution.py
+++ b/solution.py
@@ -22,10 +22,10 @@
 
 def kernel(
     seqs, secs, back, rows,
-    q_ref, k_ref, v_ref, pos_ref, res_ref, gain_ref,
+    q_ref, k_ref, v_ref, pos_ref, gain_ref,
     out_ref,
-    kv, qrot, cos_ref, sin_ref, low, acc, den, own, sent, got, gains,
-    kv_send, kv_recv, att_send, att_recv, gain_send, gain_recv,
+    q_in, k_in, pos_in, kv, qrot, cos_ref, sin_ref, low, acc, den, own, sent, got, square, gains,
+    in_sem, v_sem, kv_send, kv_recv, att_send, att_recv, gain_send, gain_recv,
 ):
     me = lax.axis_index("seq")
     sec = lax.axis_index("section")
@@ -41,6 +41,27 @@
         @pl.when(other < sec)
         def _(other=other):
             pl.semaphore_signal(barrier, inc=1, device_id={"section": other}, device_id_type=MESH)
+
+    @pl.when(sec == 2)
+    def _():
+        pl.semaphore_signal(barrier, inc=1, device_id={"section": 3}, device_id_type=MESH)
+
+    def columns(head):
+        return pl.ds(head * HD, HD)
+
+    pos_load = pltpu.make_async_copy(pos_ref, pos_in, in_sem.at[HK])
+    q_load = pltpu.make_async_copy(q_ref, q_in, in_sem.at[HK + 1])
+    gain_load = pltpu.make_async_copy(gain_ref, gains.at[secs - 1], in_sem.at[HK + 2])
+    k_loads = [
+        pltpu.make_async_copy(k_ref.at[0, :, columns(h)], k_in.at[h], in_sem.at[h])
+        for h in range(HK)
+    ]
+    v_loads = [
+        pltpu.make_async_copy(v_ref.at[0, :, columns(h)], kv.at[0, h, :, pl.ds(HD, HD)], v_sem.at[h])
+        for h in range(HK)
+    ]
+    for load in [pos_load, k_loads[0], v_loads[0], gain_load, q_load] + k_loads[1:] + v_loads[1:]:
+        load.start()
 
     def kv_copy(step, head):
         return pltpu.make_async_remote_copy(
@@ -52,12 +73,22 @@
             device_id_type=MESH,
         )
 
-    def att_copy(source, head, target):
+    def own_copy(slot, source, piece, target):
         return pltpu.make_async_remote_copy(
-            src_ref=sent.at[head],
-            dst_ref=got.at[source, head],
-            send_sem=att_send.at[target - 1, head],
-            recv_sem=att_recv.at[source, head],
+            src_ref=sent.at[piece],
+            dst_ref=got.at[source, piece],
+            send_sem=att_send.at[slot, piece],
+            recv_sem=att_recv.at[source, piece],
+            device_id={"section": target},
+            device_id_type=MESH,
+        )
+
+    def passed_copy(source, piece, target):
+        return pltpu.make_async_remote_copy(
+            src_ref=got.at[source, piece],
+            dst_ref=got.at[source, piece],
+            send_sem=att_send.at[1, piece],
+            recv_sem=att_recv.at[source, piece],
             device_id={"section": target},
             device_id_type=MESH,
         )
@@ -79,16 +110,47 @@
             def _(target=target):
                 act(target)
 
-    place = jnp.broadcast_to(pos_ref[...], (HALF, rows)).astype(jnp.float32).T
+    def send_piece(piece, act):
+        @pl.when(sec == 0)
+        def _():
+            act(own_copy(0, 0, piece, 1))
+            act(own_copy(1, 0, piece, 2))
+
+        @pl.when(sec == 1)
+        def _():
+            act(own_copy(0, 1, piece, 3))
+
+        @pl.when(sec == 2)
+        def _():
+            act(own_copy(0, 2, piece, 3))
+
+    def pass_pieces(head, act):
+        @pl.when(sec == 1)
+        def _():
+            act(passed_copy(0, GROUP * head, 3))
+
+        @pl.when(sec == 2)
+        def _():
+            act(passed_copy(0, GROUP * head + 1, 3))
+
+        @pl.when(sec == 3)
+        def _():
+            for part in range(GROUP):
+                act(passed_copy(1, GROUP * head + part, 2))
+
+    def arrive_and_go(copy):
+        copy.wait_recv()
+        copy.start()
+
+    pos_load.wait()
+    place = jnp.broadcast_to(pos_in[...], (HALF, rows)).astype(jnp.float32).T
     lane = lax.broadcasted_iota(jnp.int32, (rows, HALF), 1).astype(jnp.float32)
     angle = place * jnp.exp(lane * (-math.log(10000.0) / HALF))
     cos_ref[...] = jnp.cos(angle)
     sin_ref[...] = jnp.sin(angle)
-    gains[secs - 1] = jnp.broadcast_to(gain_ref[...], gains.shape[1:])
-
-    def turned(ref, head):
-        first = ref[0, :, head * HD : head * HD + HALF].astype(jnp.float32)
-        second = ref[0, :, head * HD + HALF : (head + 1) * HD].astype(jnp.float32)
+
+    def turned(first, second):
+        first, second = first.astype(jnp.float32), second.astype(jnp.float32)
         cosine, sine = cos_ref[...], sin_ref[...]
         return (
             (first * cosine - second * sine).astype(jnp.bfloat16),
@@ -96,13 +158,16 @@
         )
 
     def pack(head):
-        first, second = turned(k_ref, head)
+        k_loads[head].wait()
+        first, second = turned(k_in[head, :, :HALF], k_in[head, :, HALF:])
         kv[0, head, :, :HALF] = first
         kv[0, head, :, HALF:HD] = second
-        kv[0, head, :, HD:] = v_ref[0, :, head * HD : (head + 1) * HD]
+        v_loads[head].wait()
 
     pack(0)
-    expected = jnp.where(me < seqs - 1, 1, 0) + (secs - 1 - sec)
+    expected = (
+        jnp.where(me < seqs - 1, 1, 0) + (secs - 1 - sec) + jnp.where(sec == 3, 1, 0)
+    )
 
     @pl.when(expected > 0)
     def _():
@@ -112,15 +177,18 @@
     def _():
         kv_copy(0, 0).start()
 
+    gain_load.wait()
     to_later(lambda target: gain_copy(sec, target).start())
 
-    for head in range(1, HK):
-        pack(head)
+    q_load.wait()
     for head in range(HQ):
-        first, second = turned(q_ref, head)
+        at = head * HD
+        first, second = turned(q_in[0, :, at : at + HALF], q_in[0, :, at + HALF : at + HD])
         part = pl.ds((head % GROUP) * rows, rows)
         qrot[head // GROUP, part, :HALF] = first
         qrot[head // GROUP, part, HALF:] = second
+    for head in range(1, HK):
+        pack(head)
 
     reach = jnp.minimum(place, float(WINDOW - 1)).astype(jnp.int32)
     gap = lax.broadcasted_iota(jnp.int32, (rows, rows), 0) - lax.broadcasted_iota(
@@ -165,6 +233,10 @@
             def _():
                 kv_copy(0, head + 1).start()
 
+            @pl.when((step == back) & (head > 0))
+            def _():
+                pass_pieces(head - 1, arrive_and_go)
+
             @pl.when(me >= step)
             def _():
                 kv_copy(step - 1, head).wait_recv()
@@ -180,43 +252,73 @@
         lax.fori_loop(1, back + 1, earlier, 0)
         for part in range(GROUP):
             at = pl.ds(part * rows, rows)
-            cols = pl.ds(part * HD, HD)
             value = acc[at, :] / jnp.sum(den[at, :], axis=-1, keepdims=True)
-            own[head, :, cols] = value
-            sent[head, :, cols] = value.astype(jnp.bfloat16)
-        to_later(lambda target: att_copy(sec, head, target).start())
+            own[GROUP * head + part] = value
+            sent[GROUP * head + part] = value.astype(jnp.bfloat16)
+            send_piece(GROUP * head + part, lambda copy: copy.start())
         return carry
 
     lax.fori_loop(0, HK, one_head, 0)
 
-    def norm_of(parts):
-        square = 0.0
-        for head in range(HK):
-            value = parts(head)
-            square = square + jnp.sum(value * value, axis=-1, keepdims=True)
-        return lax.rsqrt(square * (1.0 / (HQ * HD)) + 1e-06)
-
-    norm = norm_of(lambda head: own[head])
-    for head in range(HK):
-        cols = slice(head * PAIR, (head + 1) * PAIR)
-        own[head] = own[head] * norm * gains[secs - 1, :1, cols] + res_ref[:, cols].astype(
-            jnp.float32
-        )
-
+    def squares(parts, pieces):
+        total = 0.0
+        for piece in pieces:
+            value = parts[piece].astype(jnp.float32)
+            value = value * value
+            for start in range(0, HD, HALF):
+                total = total + value[:, start : start + HALF]
+        return total
+
+    def norm_of(total):
+        return lax.rsqrt(
+            jnp.sum(total, axis=-1, keepdims=True) * (1.0 / (HQ * HD)) + 1e-06
+        )
+
+    norm = norm_of(squares(own, range(HQ)))
+    for piece in range(HQ):
+        own[piece] = own[piece] * norm * gains[secs - 1, :, piece * HD : (piece + 1) * HD]
+
+    def wait_piece(source, piece):
+        passed = (
+            ((sec == 1) & (source == 0) & (piece % GROUP == 0))
+            | ((sec == 2) & (source == 0) & (piece % GROUP == 1))
+            | ((sec == 3) & (source == 1))
+        )
+
+        @pl.when(jnp.logical_not(passed))
+        def _():
+            passed_copy(source, piece, 3).wait_recv()
+
+    late = range(HQ - GROUP, HQ)
+    early = range(HQ - GROUP)
     for source in range(secs - 1):
 
         @pl.when(source < sec)
         def _(source=source):
             gain_copy(source, secs - 1).wait_recv()
-            for head in range(HK):
-                att_copy(source, head, secs - 1).wait_recv()
-            norm = norm_of(lambda head: got[source, head].astype(jnp.float32))
-            for head in range(HK):
-                cols = slice(head * PAIR, (head + 1) * PAIR)
-                own[head] += got[source, head].astype(jnp.float32) * norm * gains[source, :1, cols]
-
-    for head in range(HK):
-        out_ref[0, :, head * PAIR : (head + 1) * PAIR] = own[head].astype(jnp.bfloat16)
+            for piece in early:
+                wait_piece(source, piece)
+            square[source] = squares(got.at[source], early)
+
+    pass_pieces(HK - 1, arrive_and_go)
+    for source in range(secs - 1):
+
+        @pl.when(source < sec)
+        def _(source=source):
+            for piece in late:
+                wait_piece(source, piece)
+
+    for layer in range(secs):
+
+        @pl.when(sec == layer)
+        def _(layer=layer):
+            norms = [norm_of(square[k] + squares(got.at[k], late)) for k in range(layer)]
+            for piece in range(HQ):
+                cols = slice(piece * HD, (piece + 1) * HD)
+                total = own[piece]
+                for k in range(layer):
+                    total = total + got[k, piece].astype(jnp.float32) * norms[k] * gains[k, :, cols]
+                out_ref[0, :, cols] = total.astype(jnp.bfloat16)
 
     def finish_head(head, carry):
         def finish_step(step, carry):
@@ -227,7 +329,9 @@
             return carry
 
         lax.fori_loop(0, back, finish_step, 0)
-        to_later(lambda target: att_copy(sec, head, target).wait_send())
+        for part in range(GROUP):
+            send_piece(GROUP * head + part, lambda copy: copy.wait_send())
+        pass_pieces(head, lambda copy: copy.wait_send())
         return carry
 
     lax.fori_loop(0, HK, finish_head, 0)
@@ -240,13 +344,17 @@
     secs = lax.axis_size("section")
     longest = seqs * rows // 2
     back = min((min(WINDOW, longest) - 1 + rows - 1) // rows, seqs - 1)
+    hbm = pl.BlockSpec(memory_space=pl.ANY)
     vmem = pl.BlockSpec(memory_space=pltpu.VMEM)
-    return pl.pallas_call(
+    summed = pl.pallas_call(
         functools.partial(kernel, seqs, secs, back, rows),
         out_shape=jax.ShapeDtypeStruct((1, rows, HQ * HD), jnp.bfloat16),
-        in_specs=[vmem] * 6,
+        in_specs=[hbm] * 5,
         out_specs=vmem,
         scratch_shapes=[
+            pltpu.VMEM((1, rows, HQ * HD), jnp.bfloat16),
+            pltpu.VMEM((HK, rows, HD), jnp.bfloat16),
+            pltpu.VMEM((1, rows), jnp.int32),
             pltpu.VMEM((back + 1, HK, rows, 2 * HD), jnp.bfloat16),
             pltpu.VMEM((HK, GROUP * rows, HD), jnp.bfloat16),
             pltpu.VMEM((rows, HALF), jnp.float32),
@@ -254,21 +362,26 @@
             pltpu.VMEM((rows, rows), jnp.int32),
             pltpu.VMEM((GROUP * rows, HD), jnp.float32),
             pltpu.VMEM((GROUP * rows, HALF), jnp.float32),
-            pltpu.VMEM((HK, rows, PAIR), jnp.float32),
-            pltpu.VMEM((HK, rows, PAIR), jnp.bfloat16),
-            pltpu.VMEM((secs - 1, HK, rows, PAIR), jnp.bfloat16),
-            pltpu.VMEM((secs, 8, HQ * HD), jnp.float32),
+            pltpu.VMEM((HQ, rows, HD), jnp.float32),
+            pltpu.VMEM((HQ, rows, HD), jnp.bfloat16),
+            pltpu.VMEM((secs - 1, HQ, rows, HD), jnp.bfloat16),
+            pltpu.VMEM((secs - 1, rows, HALF), jnp.float32),
+            pltpu.VMEM((secs, 1, HQ * HD), jnp.float32),
+            pltpu.SemaphoreType.DMA((HK + 3,)),
+            pltpu.SemaphoreType.DMA((HK,)),
             pltpu.SemaphoreType.DMA((back, HK)),
             pltpu.SemaphoreType.DMA((back, HK)),
-            pltpu.SemaphoreType.DMA((secs - 1, HK)),
-            pltpu.SemaphoreType.DMA((secs - 1, HK)),
+            pltpu.SemaphoreType.DMA((2, HQ)),
+            pltpu.SemaphoreType.DMA((secs - 1, HQ)),
             pltpu.SemaphoreType.DMA((secs - 1,)),
             pltpu.SemaphoreType.DMA((secs - 1,)),
         ],
         compiler_params=pltpu.CompilerParams(
             collective_id=0, has_side_effects=True, vmem_limit_bytes=52 * 2**20
         ),
-    )(queries, keys, values, positions.reshape(1, rows), residual_in, post_gain)
+    )(queries, keys, values, positions.reshape(1, rows), post_gain)
+    running = summed.astype(jnp.float32) + residual_in.astype(jnp.float32)[None]
+    return running.astype(jnp.bfloat16)
 
 
 def solution(mesh):

time: 71.3 us -> 69.8 us (0.979)
  other arithmetic: 0 us -> 2.59 us
  local copies, waits for them, and re-layouts: 5.76 us -> 3.46 us
  Pallas kernels: 64.7 us -> 63.5 us
    convert_element_type x0 -> x1, other arithmetic: none -> 2.59 us  [per_device(): return running.astype(jnp.bfloat16)]
    unnamed x9 -> x10, local copies, waits for them, and re-layouts: 5.76 us -> 3.46 us
    pallas_call x1, Pallas kernels: 64.7 us -> 63.5 us  [per_device(): pl.pallas_call(functools.partial(kernel, seqs, secs, back, rows), out_sha...]
where the time goes in v2:
time: 69.8 us; the launch traced here: 69.5 us
  Pallas kernels  63.5 us (91%)
  local copies, waits for them, and re-layouts  3.46 us (5%)
  other arithmetic  2.59 us (4%)
    pallas_call x1, Pallas kernels, per_device(): pl.pallas_call(functools.partial(kernel, seqs, secs, back, rows), out_sha...  63.5 us
    unnamed x10, local copies, waits for them, and re-layouts  3.46 us
    convert_element_type x1, other arithmetic, per_device(): return running.astype(jnp.bfloat16)  2.59 us

profile of v2, /device:TPU:28, one launch (start us, length us, event | category | flops | bytes accessed | tf_op | source)
XLA Modules:
  0.0 69.5 jit_solution(4151578599195086556)
XLA Ops:
  0.0 0.0 copy-start
  0.0 1.0 %copy-done = bf16[1,256,1024]{2,1,0:T(8,128)(2,1)S(1)} copy-done((bf16[1,256,1024]{2,1,0:T(8,128)(2,1)S(1)}, bf16[1,256,1024]{2,1,0:T(8,128)(2,1)}, u32[]{:S(2)}) %copy-start) | copy-done | bytes 524312
  1.0 0.0 copy-start.1
  1.0 1.0 %copy-done.1 = bf16[1,256,1024]{2,1,0:T(8,128)(2,1)S(1)} copy-done((bf16[1,256,1024]{2,1,0:T(8,128)(2,1)S(1)}, bf16[1,256,1024]{2,1,0:T(8,128)(2,1)}, u32[]{:S(2)}) %copy-start.1) | copy-done | bytes 524312
  2.1 0.0 copy-start.2
  2.1 0.7 copy-done.2
  2.8 0.0 copy-start.3
  2.8 0.7 copy-done.3
  3.5 0.0 copy-start.4
  3.5 63.5 %shard_map.64 = bf16[1,256,2048]{2,1,0:T(8,128)(2,1)} custom-call(bf16[1,256,2048]{2,1,0:T(8,128)(2,1)} %q_ref.1, bf16[1,256,1024]{2,1,0:T(8,128)(2,1)S(1)} %copy-done, bf16[1,256,1024]{2,1,0:T(8,128)(2,1)S(1)} %copy-done.1, s32[1,256]{1,0:T(1,128)S(1)} %bitcast.4, f32[1,2048]{1,0:T(1,128)S(1)} %copy-done.2), custom_call_target="tpu_custom_call" | custom-call | tf_op jit(solution)/shard_map/pallas_call | solution.py:349
  66.9 0.0 copy-done.4
  66.9 2.6 %fusion = bf16[1,256,2048]{2,1,0:T(8,128)(2,1)} fusion(bf16[1,256,2048]{2,1,0:T(8,128)(2,1)} %shard_map.64, bf16[256,2048]{1,0:T(8,128)(2,1)S(1)} %copy-done.4), kind=kLoop, calls=%fused_computation.1 | loop fusion | flops 2097152 | bytes 3145728 | tf_op jit(solution)/shard_map/convert_element_type | solution.py:384
Async XLA Ops:
  0.0 1.0 %copy-start = (bf16[1,256,1024]{2,1,0:T(8,128)(2,1)S(1)}, bf16[1,256,1024]{2,1,0:T(8,128)(2,1)}, u32[]{:S(2)}) copy-start(bf16[1,256,1024]{2,1,0:T(8,128)(2,1)} %k_ref.1) | copy-start | bytes 1572868
  1.0 1.0 %copy-start.1 = (bf16[1,256,1024]{2,1,0:T(8,128)(2,1)S(1)}, bf16[1,256,1024]{2,1,0:T(8,128)(2,1)}, u32[]{:S(2)}) copy-start(bf16[1,256,1024]{2,1,0:T(8,128)(2,1)} %v_ref.1) | copy-start | bytes 1572868
  2.1 0.7 %copy-start.2 = (f32[1,2048]{1,0:T(1,128)S(1)}, f32[1,2048]{1,0:T(1,128)}, u32[]{:S(2)}) copy-start(f32[1,2048]{1,0:T(1,128)} %gain_ref.1) | copy-start | bytes 24580
  2.8 0.7 copy-start.3
  3.5 63.5 %copy-start.4 = (bf16[256,2048]{1,0:T(8,128)(2,1)S(1)}, bf16[256,2048]{1,0:T(8,128)(2,1)}, u32[]{:S(2)}) copy-start(bf16[256,2048]{1,0:T(8,128)(2,1)} %param.11) | copy-start | bytes 3145732

commit v3 on v2

--- a/solution.py
+++ b/solution.py
@@ -24,8 +24,9 @@
     seqs, secs, back, rows,
     q_ref, k_ref, v_ref, pos_ref, gain_ref,
     out_ref,
-    q_in, k_in, pos_in, kv, qrot, cos_ref, sin_ref, low, acc, den, own, sent, got, square, gains,
-    in_sem, v_sem, kv_send, kv_recv, att_send, att_recv, gain_send, gain_recv,
+    q_in, k_in, pos_in, kv, qrot, cos_ref, sin_ref, low, acc, den, late_w, own, sent, got, square,
+    norms, gains,
+    in_sem, v_sem, kv_send, kv_recv, att_send, att_recv, gain_send, gain_recv, norm_send, norm_recv,
 ):
     me = lax.axis_index("seq")
     sec = lax.axis_index("section")
@@ -63,20 +64,32 @@
     for load in [pos_load, k_loads[0], v_loads[0], gain_load, q_load] + k_loads[1:] + v_loads[1:]:
         load.start()
 
-    def kv_copy(step, head):
+    def kv_copy(step, chunk):
+        if not isinstance(chunk, int) or chunk < HK - 1:
+            at = lambda block: kv.at[block, chunk]
+        elif chunk == HK - 1:
+            at = lambda block: kv.at[block, HK - 1, :, pl.ds(0, HD + HALF)]
+        else:
+            at = lambda block: kv.at[block, HK - 1, :, pl.ds(HD + HALF, HALF)]
         return pltpu.make_async_remote_copy(
-            src_ref=kv.at[step, head],
-            dst_ref=kv.at[step + 1, head],
-            send_sem=kv_send.at[step, head],
-            recv_sem=kv_recv.at[step, head],
+            src_ref=at(step),
+            dst_ref=at(step + 1),
+            send_sem=kv_send.at[step, chunk],
+            recv_sem=kv_recv.at[step, chunk],
             device_id={"seq": me + 1},
             device_id_type=MESH,
         )
 
+    def piece_of(ref, piece):
+        if not isinstance(piece, int) or piece < HQ - GROUP:
+            return ref.at[piece]
+        late = piece - (HQ - GROUP)
+        return ref.at[HQ - GROUP + late % GROUP, late // GROUP]
+
     def own_copy(slot, source, piece, target):
         return pltpu.make_async_remote_copy(
-            src_ref=sent.at[piece],
-            dst_ref=got.at[source, piece],
+            src_ref=piece_of(sent, piece),
+            dst_ref=piece_of(got.at[source], piece),
             send_sem=att_send.at[slot, piece],
             recv_sem=att_recv.at[source, piece],
             device_id={"section": target},
@@ -85,8 +98,8 @@
 
     def passed_copy(source, piece, target):
         return pltpu.make_async_remote_copy(
-            src_ref=got.at[source, piece],
-            dst_ref=got.at[source, piece],
+            src_ref=piece_of(got.at[source], piece),
+            dst_ref=piece_of(got.at[source], piece),
             send_sem=att_send.at[1, piece],
             recv_sem=att_recv.at[source, piece],
             device_id={"section": target},
@@ -99,6 +112,16 @@
             dst_ref=gains.at[source],
             send_sem=gain_send.at[target - 1],
             recv_sem=gain_recv.at[source],
+            device_id={"section": target},
+            device_id_type=MESH,
+        )
+
+    def norm_copy(source, target):
+        return pltpu.make_async_remote_copy(
+            src_ref=norms.at[secs - 1],
+            dst_ref=norms.at[source],
+            send_sem=norm_send.at[target - 1],
+            recv_sem=norm_recv.at[source],
             device_id={"section": target},
             device_id_type=MESH,
         )
@@ -197,86 +220,144 @@
     for start in range(0, rows, HALF):
         low[:, start : start + HALF] = gap[:, start : start + HALF] - reach
 
+    def weights(step, head, part, first):
+        at = pl.ds(part * rows, rows)
+        score = lax.dot_general(
+            qrot[head, at, :], kv[step, head, :, :HD], NT, preferred_element_type=jnp.float32
+        )
+        capped = jnp.tanh(score * (HD ** (-0.5) / 50.0))
+        weight = jnp.exp2(capped * (50.0 * math.log2(math.e)))
+        allowed = low[...] <= -step * rows
+        if first:
+            allowed = allowed & (gap >= 0)
+        weight = jnp.where(allowed, weight, 0.0)
+        total = weight[:, :HALF]
+        for start in range(HALF, rows, HALF):
+            total = total + weight[:, start : start + HALF]
+        if first:
+            den[at, :] = total
+        else:
+            den[at, :] += total
+        return weight.astype(jnp.bfloat16)
+
+    def add_values(weight, step, head, part, cols, first):
+        at = pl.ds(part * rows, rows)
+        summed = lax.dot_general(
+            weight,
+            kv[step, head, :, HD + cols.start : HD + cols.stop],
+            NN,
+            preferred_element_type=jnp.float32,
+        )
+        if first:
+            acc[at, cols] = summed
+        else:
+            acc[at, cols] += summed
+
     def block(step, head, first):
         for part in range(GROUP):
-            at = pl.ds(part * rows, rows)
-            score = lax.dot_general(
-                qrot[head, at, :], kv[step, head, :, :HD], NT, preferred_element_type=jnp.float32
-            )
-            capped = jnp.tanh(score * (HD ** (-0.5) / 50.0))
-            weight = jnp.exp2(capped * (50.0 * math.log2(math.e)))
-            allowed = low[...] <= -step * rows
-            if first:
-                allowed = allowed & (gap >= 0)
-            weight = jnp.where(allowed, weight, 0.0)
-            total = weight[:, :HALF]
-            for start in range(HALF, rows, HALF):
-                total = total + weight[:, start : start + HALF]
-            summed = lax.dot_general(
-                weight.astype(jnp.bfloat16),
-                kv[step, head, :, HD:],
-                NN,
-                preferred_element_type=jnp.float32,
-            )
-            if first:
-                den[at, :] = total
-                acc[at, :] = summed
-            else:
-                den[at, :] += total
-                acc[at, :] += summed
-
-    def one_head(head, carry):
-        block(0, head, True)
-
+            weight = weights(step, head, part, first)
+            add_values(weight, step, head, part, slice(0, HD), first)
+
+    def block_keep(step, first):
+        for part in range(GROUP):
+            weight = weights(step, HK - 1, part, first)
+            late_w[step, part] = weight
+            add_values(weight, step, HK - 1, part, slice(0, HALF), first)
+
+    def block_kept(step, first):
+        for part in range(GROUP):
+            add_values(late_w[step, part], step, HK - 1, part, slice(HALF, HD), first)
+
+    def start_own(chunk):
+        @pl.when(me < seqs - 1)
+        def _():
+            kv_copy(0, chunk).start()
+
+    def stream(chunk, work, last, passing):
         def earlier(step, carry):
-            @pl.when((step == back) & (head < HK - 1) & (me < seqs - 1))
-            def _():
-                kv_copy(0, head + 1).start()
-
-            @pl.when((step == back) & (head > 0))
-            def _():
-                pass_pieces(head - 1, arrive_and_go)
+            @pl.when(step == back)
+            def _():
+                last()
 
             @pl.when(me >= step)
             def _():
-                kv_copy(step - 1, head).wait_recv()
+                kv_copy(step - 1, chunk).wait_recv()
 
                 @pl.when((step < back) & (me < seqs - 1))
                 def _():
-                    kv_copy(step, head).start()
-
-                block(step, head, False)
+                    kv_copy(step, chunk).start()
+
+                work(step)
+
+            @pl.when(step == max(back - 1, 1))
+            def _():
+                passing()
 
             return carry
 
         lax.fori_loop(1, back + 1, earlier, 0)
+
+    def finish_piece(piece, part, halves):
+        at = pl.ds(part * rows, rows)
+        share = 1.0 / jnp.sum(den[at, :], axis=-1, keepdims=True)
+        total = 0.0
+        for half in halves:
+            value = acc[at, half * HALF : (half + 1) * HALF] * share
+            own[piece, half] = value
+            sent[piece, half] = value.astype(jnp.bfloat16)
+            total = total + value * value
+        square[...] += total
+
+    square[...] = jnp.zeros_like(square)
+
+    def one_head(head, carry):
+        def last():
+            @pl.when(head < HK - 2)
+            def _():
+                start_own(head + 1)
+
+            @pl.when(head == HK - 2)
+            def _():
+                start_own(HK - 1)
+
+        def passing():
+            @pl.when(head > 0)
+            def _():
+                pass_pieces(head - 1, arrive_and_go)
+
+        block(0, head, True)
+        stream(head, lambda step: block(step, head, False), last, passing)
         for part in range(GROUP):
-            at = pl.ds(part * rows, rows)
-            value = acc[at, :] / jnp.sum(den[at, :], axis=-1, keepdims=True)
-            own[GROUP * head + part] = value
-            sent[GROUP * head + part] = value.astype(jnp.bfloat16)
+            finish_piece(GROUP * head + part, part, (0, 1))
             send_piece(GROUP * head + part, lambda copy: copy.start())
         return carry
 
-    lax.fori_loop(0, HK, one_head, 0)
-
-    def squares(parts, pieces):
-        total = 0.0
-        for piece in pieces:
-            value = parts[piece].astype(jnp.float32)
-            value = value * value
-            for start in range(0, HD, HALF):
-                total = total + value[:, start : start + HALF]
-        return total
-
-    def norm_of(total):
-        return lax.rsqrt(
-            jnp.sum(total, axis=-1, keepdims=True) * (1.0 / (HQ * HD)) + 1e-06
-        )
-
-    norm = norm_of(squares(own, range(HQ)))
-    for piece in range(HQ):
-        own[piece] = own[piece] * norm * gains[secs - 1, :, piece * HD : (piece + 1) * HD]
+    lax.fori_loop(0, HK - 1, one_head, 0)
+
+    block_keep(0, True)
+    stream(
+        HK - 1,
+        lambda step: block_keep(step, False),
+        lambda: start_own(HK),
+        lambda: pass_pieces(HK - 2, arrive_and_go),
+    )
+    for part in range(GROUP):
+        finish_piece(HQ - GROUP + part, part, (0,))
+        send_piece(HQ - GROUP + part, lambda copy: copy.start())
+    block_kept(0, True)
+    stream(HK, lambda step: block_kept(step, False), lambda: None, lambda: None)
+    for part in range(GROUP):
+        finish_piece(HQ - GROUP + part, part, (1,))
+        send_piece(HQ + part, lambda copy: copy.start())
+
+    mean = jnp.sum(square[...], axis=-1, keepdims=True) * (1.0 / (HQ * HD))
+    norm = jnp.broadcast_to(lax.rsqrt(mean + 1e-06), (rows, HALF))
+    norms[secs - 1] = norm.T[:1, :]
+    to_later(lambda target: norm_copy(sec, target).start())
+    square[...] = norm
+
+    pass_pieces(HK - 1, arrive_and_go)
+    pass_pieces(HK, arrive_and_go)
 
     def wait_piece(source, piece):
         passed = (
@@ -289,53 +370,66 @@
         def _():
             passed_copy(source, piece, 3).wait_recv()
 
-    late = range(HQ - GROUP, HQ)
-    early = range(HQ - GROUP)
+    def wait_pieces(pieces):
+        for source in range(secs - 1):
+
+            @pl.when(source < sec)
+            def _(source=source):
+                for piece in pieces:
+                    wait_piece(source, piece)
+
+    def add_layers(places):
+        for layer in range(secs):
+
+            @pl.when(sec == layer)
+            def _(layer=layer):
+                spread = [
+                    jnp.broadcast_to(norms[k], (HALF, rows)).T for k in range(layer)
+                ]
+                for head, half in places:
+                    cols = slice(head * HD + half * HALF, head * HD + (half + 1) * HALF)
+                    total = own[head, half] * square[...] * gains[secs - 1, :, cols]
+                    for k in range(layer):
+                        part = got[k, head, half].astype(jnp.float32)
+                        total = total + part * spread[k] * gains[k, :, cols]
+                    out_ref[0, :, cols] = total.astype(jnp.bfloat16)
+
     for source in range(secs - 1):
 
         @pl.when(source < sec)
         def _(source=source):
             gain_copy(source, secs - 1).wait_recv()
-            for piece in early:
-                wait_piece(source, piece)
-            square[source] = squares(got.at[source], early)
-
-    pass_pieces(HK - 1, arrive_and_go)
-    for source in range(secs - 1):
-
-        @pl.when(source < sec)
-        def _(source=source):
-            for piece in late:
-                wait_piece(source, piece)
-
-    for layer in range(secs):
-
-        @pl.when(sec == layer)
-        def _(layer=layer):
-            norms = [norm_of(square[k] + squares(got.at[k], late)) for k in range(layer)]
-            for piece in range(HQ):
-                cols = slice(piece * HD, (piece + 1) * HD)
-                total = own[piece]
-                for k in range(layer):
-                    total = total + got[k, piece].astype(jnp.float32) * norms[k] * gains[k, :, cols]
-                out_ref[0, :, cols] = total.astype(jnp.bfloat16)
-
-    def finish_head(head, carry):
+            norm_copy(source, secs - 1).wait_recv()
+
+    early, late = range(HQ - GROUP), range(HQ - GROUP, HQ)
+    wait_pieces(early)
+    add_layers([(head, half) for head in early for half in (0, 1)])
+    for half in (0, 1):
+        wait_pieces(range(HQ - GROUP + half * GROUP, HQ + half * GROUP))
+        add_layers([(head, half) for head in late])
+
+    def finish(chunk):
         def finish_step(step, carry):
             @pl.when((me >= step) & (me < seqs - 1))
             def _():
-                kv_copy(step, head).wait_send()
+                kv_copy(step, chunk).wait_send()
 
             return carry
 
         lax.fori_loop(0, back, finish_step, 0)
         for part in range(GROUP):
-            send_piece(GROUP * head + part, lambda copy: copy.wait_send())
-        pass_pieces(head, lambda copy: copy.wait_send())
+            send_piece(GROUP * chunk + part, lambda copy: copy.wait_send())
+        pass_pieces(chunk, lambda copy: copy.wait_send())
+
+    def finish_head(head, carry):
+        finish(head)
         return carry
 
-    lax.fori_loop(0, HK, finish_head, 0)
+    lax.fori_loop(0, HK - 1, finish_head, 0)
+    finish(HK - 1)
+    finish(HK)
     to_later(lambda target: gain_copy(sec, target).wait_send())
+    to_later(lambda target: norm_copy(sec, target).wait_send())
 
 
 def per_device(queries, keys, values, segment_ids, positions, residual_in, post_gain):
@@ -344,11 +438,11 @@
     secs = lax.axis_size("section")
     longest = seqs * rows // 2
     back = min((min(WINDOW, longest) - 1 + rows - 1) // rows, seqs - 1)
-    hbm = pl.BlockSpec(memory_space=pl.ANY)
+    hbm = pl.BlockSpec(memory_space=pltpu.HBM)
     vmem = pl.BlockSpec(memory_space=pltpu.VMEM)
     summed = pl.pallas_call(
         functools.partial(kernel, seqs, secs, back, rows),
-        out_shape=jax.ShapeDtypeStruct((1, rows, HQ * HD), jnp.bfloat16),
+        out_shape=pltpu.VMEM((1, rows, HQ * HD), jnp.bfloat16),
         in_specs=[hbm] * 5,
         out_specs=vmem,
         scratch_shapes=[
@@ -362,22 +456,26 @@
             pltpu.VMEM((rows, rows), jnp.int32),
             pltpu.VMEM((GROUP * rows, HD), jnp.float32),
             pltpu.VMEM((GROUP * rows, HALF), jnp.float32),
-            pltpu.VMEM((HQ, rows, HD), jnp.float32),
-            pltpu.VMEM((HQ, rows, HD), jnp.bfloat16),
-            pltpu.VMEM((secs - 1, HQ, rows, HD), jnp.bfloat16),
-            pltpu.VMEM((secs - 1, rows, HALF), jnp.float32),
+            pltpu.VMEM((back + 1, GROUP, rows, rows), jnp.bfloat16),
+            pltpu.VMEM((HQ, 2, rows, HALF), jnp.float32),
+            pltpu.VMEM((HQ, 2, rows, HALF), jnp.bfloat16),
+            pltpu.VMEM((secs - 1, HQ, 2, rows, HALF), jnp.bfloat16),
+            pltpu.VMEM((rows, HALF), jnp.float32),
+            pltpu.VMEM((secs, 1, rows), jnp.float32),
             pltpu.VMEM((secs, 1, HQ * HD), jnp.float32),
             pltpu.SemaphoreType.DMA((HK + 3,)),
             pltpu.SemaphoreType.DMA((HK,)),
-            pltpu.SemaphoreType.DMA((back, HK)),
-            pltpu.SemaphoreType.DMA((back, HK)),
-            pltpu.SemaphoreType.DMA((2, HQ)),
-            pltpu.SemaphoreType.DMA((secs - 1, HQ)),
+            pltpu.SemaphoreType.DMA((back, HK + 1)),
+            pltpu.SemaphoreType.DMA((back, HK + 1)),
+            pltpu.SemaphoreType.DMA((2, HQ + GROUP)),
+            pltpu.SemaphoreType.DMA((secs - 1, HQ + GROUP)),
+            pltpu.SemaphoreType.DMA((secs - 1,)),
+            pltpu.SemaphoreType.DMA((secs - 1,)),
             pltpu.SemaphoreType.DMA((secs - 1,)),
             pltpu.SemaphoreType.DMA((secs - 1,)),
         ],
         compiler_params=pltpu.CompilerParams(
-            collective_id=0, has_side_effects=True, vmem_limit_bytes=52 * 2**20
+            collective_id=0, has_side_effects=True, vmem_limit_bytes=60 * 2**20
         ),
     )(queries, keys, values, positions.reshape(1, rows), post_gain)
     running = summed.astype(jnp.float32) + residual_in.astype(jnp.float32)[None]

time: 69.8 us -> 62.4 us (0.89)
  local copies, waits for them, and re-layouts: 3.46 us -> 0.01 us
  Pallas kernels: 63.5 us -> 60.8 us
  other arithmetic: 2.59 us -> 1.36 us
    unnamed x10 -> x2, local copies, waits for them, and re-layouts: 3.46 us -> 0.01 us
    pallas_call x1, Pallas kernels: 63.5 us -> 60.8 us  [per_device(): pl.pallas_call(functools.partial(kernel, seqs, secs, back, rows), out_sha...]
    convert_element_type x1, other arithmetic: 2.59 us -> 1.36 us  [per_device(): return running.astype(jnp.bfloat16)]
where the time goes in v3:
time: 62.4 us; the launch traced here: 62.2 us
  Pallas kernels  60.8 us (97%)
  other arithmetic  1.36 us (2%)
    pallas_call x1, Pallas kernels, per_device(): pl.pallas_call(functools.partial(kernel, seqs, secs, back, rows), out_sha...  60.8 us
    convert_element_type x1, other arithmetic, per_device(): return running.astype(jnp.bfloat16)  1.36 us

profile of v3, /device:TPU:28, one launch (start us, length us, event | category | flops | bytes accessed | tf_op | source)
XLA Modules:
  0.0 62.2 jit_solution(1456122821398652479)
XLA Ops:
  0.0 0.0 copy-start
  0.0 60.8 %shard_map.64 = bf16[1,256,2048]{2,1,0:T(8,128)(2,1)S(1)} custom-call(bf16[1,256,2048]{2,1,0:T(8,128)(2,1)} %q_ref.1, bf16[1,256,1024]{2,1,0:T(8,128)(2,1)} %k_ref.1, bf16[1,256,1024]{2,1,0:T(8,128)(2,1)} %v_ref.1, s32[1,256]{1,0:T(1,128)} %bitcast.4, f32[1,2048]{1,0:T(1,128)} %gain_ref.1), custom_call_target="tpu_custom_call" | custom-call | tf_op jit(solution)/shard_map/pallas_call | solution.py:443
  60.8 0.0 copy-done
  60.8 1.4 %fusion = bf16[1,256,2048]{2,1,0:T(8,128)(2,1)} fusion(bf16[1,256,2048]{2,1,0:T(8,128)(2,1)S(1)} %shard_map.64, bf16[256,2048]{1,0:T(8,128)(2,1)S(1)} %copy-done), kind=kLoop, calls=%fused_computation.1 | loop fusion | flops 2097152 | bytes 3145728 | tf_op jit(solution)/shard_map/convert_element_type | solution.py:482
Async XLA Ops:
  0.0 60.8 %copy-start = (bf16[256,2048]{1,0:T(8,128)(2,1)S(1)}, bf16[256,2048]{1,0:T(8,128)(2,1)}, u32[]{:S(2)}) copy-start(bf16[256,2048]{1,0:T(8,128)(2,1)} %param.11) | copy-start | bytes 3145732

commit v4 on v3

--- a/solution.py
+++ b/solution.py
@@ -31,11 +31,16 @@
     me = lax.axis_index("seq")
     sec = lax.axis_index("section")
 
+    even = lax.rem(me, 2) == 0
     barrier = pltpu.get_barrier_semaphore()
 
     @pl.when(me > 0)
     def _():
         pl.semaphore_signal(barrier, inc=1, device_id={"seq": me - 1}, device_id_type=MESH)
+
+    @pl.when(even & (me > 1))
+    def _():
+        pl.semaphore_signal(barrier, inc=1, device_id={"seq": me - 2}, device_id_type=MESH)
 
     for other in range(secs - 1):
 
@@ -64,7 +69,7 @@
     for load in [pos_load, k_loads[0], v_loads[0], gain_load, q_load] + k_loads[1:] + v_loads[1:]:
         load.start()
 
-    def kv_copy(step, chunk):
+    def kv_copy(step, chunk, by=1):
         if not isinstance(chunk, int) or chunk < HK - 1:
             at = lambda block: kv.at[block, chunk]
         elif chunk == HK - 1:
@@ -73,12 +78,21 @@
             at = lambda block: kv.at[block, HK - 1, :, pl.ds(HD + HALF, HALF)]
         return pltpu.make_async_remote_copy(
             src_ref=at(step),
-            dst_ref=at(step + 1),
-            send_sem=kv_send.at[step, chunk],
-            recv_sem=kv_recv.at[step, chunk],
-            device_id={"seq": me + 1},
+            dst_ref=at(step + by),
+            send_sem=kv_send.at[by - 1, step, chunk],
+            recv_sem=kv_recv.at[step + by - 1, chunk],
+            device_id={"seq": me + by},
             device_id_type=MESH,
         )
+
+    def send_block(step, chunk, act):
+        @pl.when(even & (me + 2 < seqs) & (step + 2 <= back))
+        def _():
+            act(kv_copy(step, chunk, 2))
+
+        @pl.when((even | (step == 0)) & (me + 1 < seqs) & (step + 1 <= back))
+        def _():
+            act(kv_copy(step, chunk, 1))
 
     def piece_of(ref, piece):
         if not isinstance(piece, int) or piece < HQ - GROUP:
@@ -189,16 +203,17 @@
 
     pack(0)
     expected = (
-        jnp.where(me < seqs - 1, 1, 0) + (secs - 1 - sec) + jnp.where(sec == 3, 1, 0)
+        jnp.where(me < seqs - 1, 1, 0)
+        + jnp.where(even & (me + 2 < seqs), 1, 0)
+        + (secs - 1 - sec)
+        + jnp.where(sec == 3, 1, 0)
     )
 
     @pl.when(expected > 0)
     def _():
         pl.semaphore_wait(barrier, expected)
 
-    @pl.when(me < seqs - 1)
-    def _():
-        kv_copy(0, 0).start()
+    send_block(0, 0, lambda copy: copy.start())
 
     gain_load.wait()
     to_later(lambda target: gain_copy(sec, target).start())
@@ -269,9 +284,7 @@
             add_values(late_w[step, part], step, HK - 1, part, slice(HALF, HD), first)
 
     def start_own(chunk):
-        @pl.when(me < seqs - 1)
-        def _():
-            kv_copy(0, chunk).start()
+        send_block(0, chunk, lambda copy: copy.start())
 
     def stream(chunk, work, last, passing):
         def earlier(step, carry):
@@ -283,10 +296,7 @@
             def _():
                 kv_copy(step - 1, chunk).wait_recv()
 
-                @pl.when((step < back) & (me < seqs - 1))
-                def _():
-                    kv_copy(step, chunk).start()
-
+                send_block(step, chunk, lambda copy: copy.start())
                 work(step)
 
             @pl.when(step == max(back - 1, 1))
@@ -410,9 +420,9 @@
 
     def finish(chunk):
         def finish_step(step, carry):
-            @pl.when((me >= step) & (me < seqs - 1))
-            def _():
-                kv_copy(step, chunk).wait_send()
+            @pl.when(me >= step)
+            def _():
+                send_block(step, chunk, lambda copy: copy.wait_send())
 
             return carry
 
@@ -465,7 +475,7 @@
             pltpu.VMEM((secs, 1, HQ * HD), jnp.float32),
             pltpu.SemaphoreType.DMA((HK + 3,)),
             pltpu.SemaphoreType.DMA((HK,)),
-            pltpu.SemaphoreType.DMA((back, HK + 1)),
+            pltpu.SemaphoreType.DMA((2, back, HK + 1)),
             pltpu.SemaphoreType.DMA((back, HK + 1)),
             pltpu.SemaphoreType.DMA((2, HQ + GROUP)),
             pltpu.SemaphoreType.DMA((secs - 1, HQ + GROUP)),

time: 62.4 us -> 66 us (1.058)
  Pallas kernels: 60.8 us -> 64.5 us
    pallas_call x1, Pallas kernels: 60.8 us -> 64.5 us  [per_device(): pl.pallas_call(functools.partial(kernel, seqs, secs, back, rows), out_sha...]
where the time goes in v4:
time: 66 us; the launch traced here: 65.9 us
  Pallas kernels  64.5 us (98%)
  other arithmetic  1.36 us (2%)
    pallas_call x1, Pallas kernels, per_device(): pl.pallas_call(functools.partial(kernel, seqs, secs, back, rows), out_sha...  64.5 us
    convert_element_type x1, other arithmetic, per_device(): return running.astype(jnp.bfloat16)  1.36 us

profile of v4, /device:TPU:28, one launch (start us, length us, event | category | flops | bytes accessed | tf_op | source)
XLA Modules:
  0.0 65.9 jit_solution(6672502014806293554)
XLA Ops:
  0.0 0.0 copy-start
  0.0 64.5 %shard_map.64 = bf16[1,256,2048]{2,1,0:T(8,128)(2,1)S(1)} custom-call(bf16[1,256,2048]{2,1,0:T(8,128)(2,1)} %q_ref.1, bf16[1,256,1024]{2,1,0:T(8,128)(2,1)} %k_ref.1, bf16[1,256,1024]{2,1,0:T(8,128)(2,1)} %v_ref.1, s32[1,256]{1,0:T(1,128)} %bitcast.4, f32[1,2048]{1,0:T(1,128)} %gain_ref.1), custom_call_target="tpu_custom_call" | custom-call | tf_op jit(solution)/shard_map/pallas_call | solution.py:453
  64.5 0.0 copy-done
  64.5 1.4 %fusion = bf16[1,256,2048]{2,1,0:T(8,128)(2,1)} fusion(bf16[1,256,2048]{2,1,0:T(8,128)(2,1)S(1)} %shard_map.64, bf16[256,2048]{1,0:T(8,128)(2,1)S(1)} %copy-done), kind=kLoop, calls=%fused_computation.1 | loop fusion | flops 2097152 | bytes 3145728 | tf_op jit(solution)/shard_map/convert_element_type | solution.py:492
Async XLA Ops:
  0.0 64.5 %copy-start = (bf16[256,2048]{1,0:T(8,128)(2,1)S(1)}, bf16[256,2048]{1,0:T(8,128)(2,1)}, u32[]{:S(2)}) copy-start(bf16[256,2048]{1,0:T(8,128)(2,1)} %param.11) | copy-start | bytes 3145732

commit v5 on v3

--- a/solution.py
+++ b/solution.py
@@ -18,6 +18,28 @@
 MESH = pl.DeviceIdType.MESH
 NT = (((1,), (1,)), ((), ()))
 NN = (((1,), (0,)), ((), ()))
+
+
+def cos_sin(angle):
+    turns = jnp.floor(angle * (2.0 / math.pi) + 0.5)
+    rest = angle - turns * 1.5703125
+    rest = rest - turns * 4.837512969970703125e-4
+    rest = rest - turns * 7.549789948768648e-8
+    z = rest * rest
+    sine = rest + rest * z * (
+        -1.6666654611e-1 + z * (8.3321608736e-3 + z * -1.9515295891e-4)
+    )
+    cosine = (1.0 - 0.5 * z) + z * z * (
+        4.166664568298827e-2 + z * (-1.388731625493765e-3 + z * 2.443315711809948e-5)
+    )
+    quarter = turns.astype(jnp.int32) & 3
+    odd = (quarter & 1) == 1
+    first = jnp.where(odd, sine, cosine)
+    second = jnp.where(odd, cosine, sine)
+    return (
+        jnp.where((quarter == 1) | (quarter == 2), -first, first),
+        jnp.where(quarter >= 2, -second, second),
+    )
 
 
 def kernel(
@@ -169,8 +191,7 @@
     place = jnp.broadcast_to(pos_in[...], (HALF, rows)).astype(jnp.float32).T
     lane = lax.broadcasted_iota(jnp.int32, (rows, HALF), 1).astype(jnp.float32)
     angle = place * jnp.exp(lane * (-math.log(10000.0) / HALF))
-    cos_ref[...] = jnp.cos(angle)
-    sin_ref[...] = jnp.sin(angle)
+    cos_ref[...], sin_ref[...] = cos_sin(angle)
 
     def turned(first, second):
         first, second = first.astype(jnp.float32), second.astype(jnp.float32)
@@ -218,12 +239,14 @@
         jnp.int32, (rows, rows), 1
     )
     for start in range(0, rows, HALF):
-        low[:, start : start + HALF] = gap[:, start : start + HALF] - reach
-
-    def weights(step, head, part, first):
-        at = pl.ds(part * rows, rows)
+        part = gap[:, start : start + HALF] - reach
+        for at in range(0, GROUP * rows, rows):
+            low[at : at + rows, start : start + HALF] = part
+    gap = jnp.concatenate([gap] * GROUP, axis=0)
+
+    def weights(step, head, first):
         score = lax.dot_general(
-            qrot[head, at, :], kv[step, head, :, :HD], NT, preferred_element_type=jnp.float32
+            qrot[head], kv[step, head, :, :HD], NT, preferred_element_type=jnp.float32
         )
         capped = jnp.tanh(score * (HD ** (-0.5) / 50.0))
         weight = jnp.exp2(capped * (50.0 * math.log2(math.e)))
@@ -235,13 +258,12 @@
         for start in range(HALF, rows, HALF):
             total = total + weight[:, start : start + HALF]
         if first:
-            den[at, :] = total
+            den[...] = total
         else:
-            den[at, :] += total
+            den[...] += total
         return weight.astype(jnp.bfloat16)
 
-    def add_values(weight, step, head, part, cols, first):
-        at = pl.ds(part * rows, rows)
+    def add_values(weight, step, head, cols, first):
         summed = lax.dot_general(
             weight,
             kv[step, head, :, HD + cols.start : HD + cols.stop],
@@ -249,24 +271,20 @@
             preferred_element_type=jnp.float32,
         )
         if first:
-            acc[at, cols] = summed
+            acc[:, cols] = summed
         else:
-            acc[at, cols] += summed
+            acc[:, cols] += summed
 
     def block(step, head, first):
-        for part in range(GROUP):
-            weight = weights(step, head, part, first)
-            add_values(weight, step, head, part, slice(0, HD), first)
+        add_values(weights(step, head, first), step, head, slice(0, HD), first)
 
     def block_keep(step, first):
-        for part in range(GROUP):
-            weight = weights(step, HK - 1, part, first)
-            late_w[step, part] = weight
-            add_values(weight, step, HK - 1, part, slice(0, HALF), first)
+        weight = weights(step, HK - 1, first)
+        late_w[step] = weight
+        add_values(weight, step, HK - 1, slice(0, HALF), first)
 
     def block_kept(step, first):
-        for part in range(GROUP):
-            add_values(late_w[step, part], step, HK - 1, part, slice(HALF, HD), first)
+        add_values(late_w[step], step, HK - 1, slice(HALF, HD), first)
 
     def start_own(chunk):
         @pl.when(me < seqs - 1)
@@ -453,10 +471,10 @@
             pltpu.VMEM((HK, GROUP * rows, HD), jnp.bfloat16),
             pltpu.VMEM((rows, HALF), jnp.float32),
             pltpu.VMEM((rows, HALF), jnp.float32),
-            pltpu.VMEM((rows, rows), jnp.int32),
+            pltpu.VMEM((GROUP * rows, rows), jnp.int32),
             pltpu.VMEM((GROUP * rows, HD), jnp.float32),
             pltpu.VMEM((GROUP * rows, HALF), jnp.float32),
-            pltpu.VMEM((back + 1, GROUP, rows, rows), jnp.bfloat16),
+            pltpu.VMEM((back + 1, GROUP * rows, rows), jnp.bfloat16),
             pltpu.VMEM((HQ, 2, rows, HALF), jnp.float32),
             pltpu.VMEM((HQ, 2, rows, HALF), jnp.bfloat16),
             pltpu.VMEM((secs - 1, HQ, 2, rows, HALF), jnp.bfloat16),

time: 62.4 us -> 62.2 us (level)
  no operation moved by 1% of the time
where the time goes in v5:
time: 62.2 us; the launch traced here: 62.1 us
  Pallas kernels  60.7 us (98%)
  other arithmetic  1.36 us (2%)
    pallas_call x1, Pallas kernels, per_device(): pl.pallas_call(functools.partial(kernel, seqs, secs, back, rows), out_sha...  60.7 us
    convert_element_type x1, other arithmetic, per_device(): return running.astype(jnp.bfloat16)  1.36 us

profile of v5, /device:TPU:28, one launch (start us, length us, event | category | flops | bytes accessed | tf_op | source)
XLA Modules:
  0.0 62.1 jit_solution(6108896046284636136)
XLA Ops:
  0.0 0.0 copy-start
  0.0 60.7 %shard_map.64 = bf16[1,256,2048]{2,1,0:T(8,128)(2,1)S(1)} custom-call(bf16[1,256,2048]{2,1,0:T(8,128)(2,1)} %q_ref.1, bf16[1,256,1024]{2,1,0:T(8,128)(2,1)} %k_ref.1, bf16[1,256,1024]{2,1,0:T(8,128)(2,1)} %v_ref.1, s32[1,256]{1,0:T(1,128)} %bitcast.4, f32[1,2048]{1,0:T(1,128)} %gain_ref.1), custom_call_target="tpu_custom_call" | custom-call | tf_op jit(solution)/shard_map/pallas_call | solution.py:461
  60.7 0.0 copy-done
  60.7 1.4 %fusion = bf16[1,256,2048]{2,1,0:T(8,128)(2,1)} fusion(bf16[1,256,2048]{2,1,0:T(8,128)(2,1)S(1)} %shard_map.64, bf16[256,2048]{1,0:T(8,128)(2,1)S(1)} %copy-done), kind=kLoop, calls=%fused_computation.1 | loop fusion | flops 2097152 | bytes 3145728 | tf_op jit(solution)/shard_map/convert_element_type | solution.py:500
Async XLA Ops:
  0.0 60.7 %copy-start = (bf16[256,2048]{1,0:T(8,128)(2,1)S(1)}, bf16[256,2048]{1,0:T(8,128)(2,1)}, u32[]{:S(2)}) copy-start(bf16[256,2048]{1,0:T(8,128)(2,1)} %param.11) | copy-start | bytes 3145732

commit v6 on v5

--- a/solution.py
+++ b/solution.py
@@ -352,18 +352,58 @@
 
     lax.fori_loop(0, HK - 1, one_head, 0)
 
+    def late_arrives(step):
+        kv_copy(step - 1, HK).wait_recv()
+
+        @pl.when((step < back) & (me < seqs - 1))
+        def _():
+            kv_copy(step, HK).start()
+
+    def last_head(step, carry):
+        @pl.when(me >= step)
+        def _():
+            kv_copy(step - 1, HK - 1).wait_recv()
+
+            @pl.when((step < back) & (me < seqs - 1))
+            def _():
+                kv_copy(step, HK - 1).start()
+
+        @pl.when(step == 1)
+        def _():
+            start_own(HK)
+
+        @pl.when((step > 1) & (me >= step - 1))
+        def _():
+            late_arrives(step - 1)
+
+        @pl.when(me >= step)
+        def _():
+            block_keep(step, False)
+
+        @pl.when(step == max(back - 1, 1))
+        def _():
+            pass_pieces(HK - 2, arrive_and_go)
+
+        return carry
+
+    def last_values(step, carry):
+        @pl.when((step == back) & (me >= step))
+        def _():
+            late_arrives(step)
+
+        @pl.when(me >= step)
+        def _():
+            block_kept(step, False)
+
+        return carry
+
     block_keep(0, True)
-    stream(
-        HK - 1,
-        lambda step: block_keep(step, False),
-        lambda: start_own(HK),
-        lambda: pass_pieces(HK - 2, arrive_and_go),
-    )
+    lax.fori_loop(1, back + 1, last_head, 0)
     for part in range(GROUP):
         finish_piece(HQ - GROUP + part, part, (0,))
         send_piece(HQ - GROUP + part, lambda copy: copy.start())
     block_kept(0, True)
-    stream(HK, lambda step: block_kept(step, False), lambda: None, lambda: None)
+    lax.fori_loop(1, back + 1, last_values, 0)
     for part in range(GROUP):
         finish_piece(HQ - GROUP + part, part, (1,))
         send_piece(HQ + part, lambda copy: copy.start())

time: 62.2 us -> 62 us (level)
  no operation moved by 1% of the time
where the time goes in v6:
time: 62 us; the launch traced here: 61.8 us
  Pallas kernels  60.4 us (97%)
  other arithmetic  1.36 us (2%)
    pallas_call x1, Pallas kernels, per_device(): pl.pallas_call(functools.partial(kernel, seqs, secs, back, rows), out_sha...  60.4 us
    convert_element_type x1, other arithmetic, per_device(): return running.astype(jnp.bfloat16)  1.36 us

profile of v6, /device:TPU:28, one launch (start us, length us, event | category | flops | bytes accessed | tf_op | source)
XLA Modules:
  0.0 61.8 jit_solution(12621967165994104864)
XLA Ops:
  0.0 0.0 copy-start
  0.0 60.4 %shard_map.64 = bf16[1,256,2048]{2,1,0:T(8,128)(2,1)S(1)} custom-call(bf16[1,256,2048]{2,1,0:T(8,128)(2,1)} %q_ref.1, bf16[1,256,1024]{2,1,0:T(8,128)(2,1)} %k_ref.1, bf16[1,256,1024]{2,1,0:T(8,128)(2,1)} %v_ref.1, s32[1,256]{1,0:T(1,128)} %bitcast.4, f32[1,2048]{1,0:T(1,128)} %gain_ref.1), custom_call_target="tpu_custom_call" | custom-call | tf_op jit(solution)/shard_map/pallas_call | solution.py:501
  60.4 0.0 copy-done
  60.5 1.4 %fusion = bf16[1,256,2048]{2,1,0:T(8,128)(2,1)} fusion(bf16[1,256,2048]{2,1,0:T(8,128)(2,1)S(1)} %shard_map.64, bf16[256,2048]{1,0:T(8,128)(2,1)S(1)} %copy-done), kind=kLoop, calls=%fused_computation.1 | loop fusion | flops 2097152 | bytes 3145728 | tf_op jit(solution)/shard_map/convert_element_type | solution.py:540
Async XLA Ops:
  0.0 60.4 %copy-start = (bf16[256,2048]{1,0:T(8,128)(2,1)S(1)}, bf16[256,2048]{1,0:T(8,128)(2,1)}, u32[]{:S(2)}) copy-start(bf16[256,2048]{1,0:T(8,128)(2,1)} %param.11) | copy-start | bytes 3145732
